TPU v7x, 32 devices: a whole 2x2x4 slice. The times are simulated.
32 devices in a mesh: seq: 16 (over z, x, core), heads: 2 (over y).
Axes of the slice: x: 2, y: 2, z: 4, core: 2. Of those that a mesh axis runs over, the one named last changes fastest.
Arguments:
- tokens: bfloat16 [16384, 768], P('seq'), may hold values from -6 to 6
- cotangent: float32 [16384, 768], P('seq'), may hold values from -6 to 6
- valid_tiles: int32 [16384], P('seq'), may hold values from 0 to 1, as said below
- gain_first: float32 [768], replicated, may hold values from 0.25 to 1.75
- shift_first: float32 [768], replicated, may hold values from -4 to 4
- w_project: bfloat16 [768, 3, 768], P(None, None, 'heads'), may hold values from -0.21875 to 0.21875
- bias_project: float32 [2, 768], P(None, 'heads'), may hold values from -0.3125 to 0.3125
- w_output: bfloat16 [768, 768], P('heads'), may hold values from -4 to 4
- bias_output: float32 [768], replicated, may hold values from -4 to 4
- gain_second: float32 [768], replicated, may hold values from 0.25 to 1.75
- shift_second: float32 [768], replicated, may hold values from -4 to 4
- w_expand: bfloat16 [768, 3072], P(None, 'heads'), may hold values from -0.21875 to 0.21875
- bias_expand: float32 [3072], P('heads'), may hold values from -4 to 4
- w_reduce: bfloat16 [3072, 768], P('heads'), may hold values from -0.109375 to 0.109375
- bias_reduce: float32 [768], replicated, may hold values from -4 to 4
Outputs:
- layer_out: float32 [16384, 768], P('seq')
- grad_tokens: float32 [16384, 768], P('seq')
- grad_gain_first: float32 [768], replicated
- grad_shift_first: float32 [768], replicated
- grad_w_project: float32 [768, 3, 768], P(None, None, 'heads')
- grad_bias_project: float32 [2, 768], P(None, 'heads')
- grad_w_output: float32 [768, 768], P('heads')
- grad_bias_output: float32 [768], replicated
- grad_gain_second: float32 [768], replicated
- grad_shift_second: float32 [768], replicated
- grad_w_expand: float32 [768, 3072], P(None, 'heads')
- grad_bias_expand: float32 [3072], P('heads')
- grad_w_reduce: float32 [3072, 768], P('heads')
- grad_bias_reduce: float32 [768], replicated
Inputs may be any that keep to these rules, and one draw needn't show every extreme that they name: `valid_tiles`: in each aligned run of 16384 tiles the valid ones come first and at least one is valid; in some run more than 15360 are valid and at least one is padding.
All inputs are finite; a program needn't handle non-finite values.
Results may differ from a plain program's by a relative error of at most 0.02.
Values may be sent and summed in bfloat16 or wider, within the bound.
A program may use at most 256 MiB of HBM per device.

v0:
```python
import jax
import jax.numpy as jnp
from jax import lax
from jax.sharding import PartitionSpec as P

HEADS = 16
HEAD_DIM = 48
SEGMENT = 1024
BRANCHES = 5


masked_score = -1000000000.0
absent_top = -1e30
layer_eps = 1e-05


def as_sent(value):
    return jax.tree.map(lambda a: a.astype(jnp.bfloat16) if a.dtype == jnp.float32 else a, value)


def passed_along(value, axis, by):
    peers = lax.axis_size(axis)
    pairs = [(i, i + by) for i in range(peers) if 0 <= i + by < peers]
    return lax.ppermute(value, axis, pairs)


def norm_rows(values, gain, shift):
    mean_row = jnp.mean(values, axis=-1, keepdims=True)
    centered = values - mean_row
    variance = jnp.mean(centered * centered, axis=-1, keepdims=True)
    return centered * lax.rsqrt(variance + layer_eps) * gain + shift


def gelu_tanh(values):
    return jax.nn.gelu(values, approximate=True)


def head_choice(stride, local_heads):
    owned = lax.axis_index("heads") * local_heads + jnp.arange(local_heads, dtype=jnp.int32)
    return jnp.arange(stride, dtype=jnp.int32)[:, None] == (owned % stride)[None, :]


def pick(rows, chosen):
    stride = chosen.shape[0]
    shaped = rows.reshape((rows.shape[0] // stride, stride) + rows.shape[1:])
    if rows.ndim == 1:
        shaped = jnp.broadcast_to(shaped[:, :, None], shaped.shape + (chosen.shape[1],))
        marker = chosen[None]
    else:
        marker = chosen.reshape((1,) + chosen.shape + (1,) * (rows.ndim - 2))
    return jnp.sum(jnp.where(marker, shaped, jnp.zeros((), rows.dtype)), axis=1)


def spread(branch_part, chosen, filler):
    stride = chosen.shape[0]
    marker = chosen.reshape((1,) + chosen.shape + (1,) * (branch_part.ndim - 2))
    expanded = jnp.where(marker, branch_part[:, None], jnp.asarray(filler, branch_part.dtype))
    return expanded.reshape((branch_part.shape[0] * stride,) + branch_part.shape[1:])


def to_pieces(array):
    row_count, local_heads = (array.shape[0], array.shape[1])
    shaped = array.reshape((row_count // SEGMENT, SEGMENT, local_heads) + array.shape[2:])
    shaped = jnp.swapaxes(shaped, 1, 2)
    return shaped.reshape((shaped.shape[0] * local_heads, SEGMENT, 1) + array.shape[2:])


def from_pieces(pieces, local_heads):
    shaped = pieces.reshape((-1, local_heads, SEGMENT) + pieces.shape[3:])
    shaped = jnp.swapaxes(shaped, 1, 2)
    return shaped.reshape((shaped.shape[0] * SEGMENT, local_heads) + pieces.shape[3:])


def fresh_state(row_count, local_heads):
    return (
        jnp.full((row_count, local_heads), absent_top, jnp.float32),
        jnp.zeros((row_count, local_heads), jnp.float32),
        jnp.zeros((row_count, local_heads, HEAD_DIM), jnp.float32),
    )


def merge_state(running, branch_part):
    new_top = jnp.maximum(running[0], branch_part[0])
    left_scale = jnp.exp(running[0] - new_top)
    right_scale = jnp.exp(branch_part[0] - new_top)
    row_total = running[1] * left_scale + branch_part[1] * right_scale
    weighted = running[2] * left_scale[:, :, None] + branch_part[2] * right_scale[:, :, None]
    return (new_top, row_total, weighted)


def attend_step(queries, key_rows, value_rows, key_valid, running):
    row_top, row_total, weighted = running
    scores = jnp.einsum(
        "qhe,khe->hqk", queries, key_rows, preferred_element_type=jnp.float32
    ) * HEAD_DIM ** (-0.5)
    scores = jnp.where(jnp.transpose(key_valid)[:, None, :] > 0, scores, masked_score)
    new_top = jnp.maximum(row_top, jnp.transpose(jnp.max(scores, axis=-1)))
    raised = jnp.exp(scores - jnp.transpose(new_top)[:, :, None])
    rescale = jnp.exp(row_top - new_top)
    row_total = row_total * rescale + jnp.transpose(jnp.sum(raised, axis=-1))
    weighted = weighted * rescale[:, :, None] + jnp.einsum(
        "hqk,khe->qhe", raised.astype(jnp.bfloat16), value_rows, preferred_element_type=jnp.float32
    )
    return (new_top, row_total, weighted)


def attend_back(queries, key_rows, value_rows, key_valid, grad_attn, delta, row_top, row_total):
    score_scale = HEAD_DIM ** (-0.5)
    scores = (
        jnp.einsum("qhe,khe->hqk", queries, key_rows, preferred_element_type=jnp.float32)
        * score_scale
    )
    live = jnp.transpose(key_valid)[:, None, :] > 0
    scores = jnp.where(live, scores, masked_score)
    probs = (
        jnp.exp(scores - jnp.transpose(row_top)[:, :, None]) / jnp.transpose(row_total)[:, :, None]
    )
    grad_values = jnp.einsum(
        "hqk,qhe->khe", probs.astype(jnp.bfloat16), grad_attn, preferred_element_type=jnp.float32
    )
    grad_probs = jnp.einsum(
        "qhe,khe->hqk", grad_attn, value_rows, preferred_element_type=jnp.float32
    )
    grad_scores = jnp.where(
        live, probs * (grad_probs - jnp.transpose(delta)[:, :, None]), 0.0
    ).astype(jnp.bfloat16)
    grad_queries = (
        jnp.einsum("hqk,khe->qhe", grad_scores, key_rows, preferred_element_type=jnp.float32)
        * score_scale
    )
    grad_keys = (
        jnp.einsum("hqk,qhe->khe", grad_scores, queries, preferred_element_type=jnp.float32)
        * score_scale
    )
    return (grad_queries, grad_keys, grad_values)


def local_forward(selected):
    local_heads = selected[0].shape[1]

    def one_piece(pieces):
        return attend_step(pieces[0], pieces[1], pieces[2], pieces[3], fresh_state(SEGMENT, 1))

    results = lax.map(one_piece, tuple((to_pieces(entry) for entry in selected)))
    return tuple((from_pieces(entry, local_heads) for entry in results))


def local_backward(selected):
    local_heads = selected[0].shape[1]

    def one_piece(pieces):
        return attend_back(*pieces)

    results = lax.map(one_piece, tuple((to_pieces(entry) for entry in selected)))
    return tuple((from_pieces(entry, local_heads) for entry in results))


def relay_forward(selected, members):
    position = lax.axis_index("seq") % members
    queries = selected[0]
    travel = selected[1:]
    running = attend_step(
        queries, travel[0], travel[1], travel[2], fresh_state(queries.shape[0], queries.shape[1])
    )

    def turn(turn_index, carry_pack):
        running, travel = carry_pack
        onward = jax.tree.map(
            lambda part, own: part.astype(own.dtype),
            passed_along(as_sent(travel), "seq", 1),
            travel,
        )
        beside_all = jax.tree.map(
            lambda part, own: part.astype(own.dtype),
            passed_along(as_sent(travel), "seq", 1 - members),
            travel,
        )
        travel = jax.tree.map(
            lambda near_piece, far_piece: jnp.where(position == 0, far_piece, near_piece),
            onward,
            beside_all,
        )
        return (attend_step(queries, travel[0], travel[1], travel[2], running), travel)

    running, travel = lax.fori_loop(0, members - 1, turn, (running, travel))
    return running


def relay_backward(selected, members):
    position = lax.axis_index("seq") % members
    queries, key_rows, value_rows, key_valid, grad_attn, delta, row_top, row_total = selected
    travel = (
        key_rows,
        value_rows,
        key_valid,
        jnp.zeros(key_rows.shape, jnp.float32),
        jnp.zeros(value_rows.shape, jnp.float32),
    )

    def turn(turn_index, carry_pack):
        grad_queries, travel = carry_pack
        part_queries, part_keys, part_values = attend_back(
            queries, travel[0], travel[1], travel[2], grad_attn, delta, row_top, row_total
        )
        travel = (travel[0], travel[1], travel[2], travel[3] + part_keys, travel[4] + part_values)
        onward = (
            passed_along(travel[0], "seq", 1),
            passed_along(travel[1], "seq", 1),
            passed_along(travel[2], "seq", 1),
            passed_along(travel[3].astype(jnp.bfloat16), "seq", 1).astype(jnp.float32),
            passed_along(travel[4].astype(jnp.bfloat16), "seq", 1).astype(jnp.float32),
        )
        beside_all = (
            passed_along(travel[0], "seq", 1 - members),
            passed_along(travel[1], "seq", 1 - members),
            passed_along(travel[2], "seq", 1 - members),
            passed_along(travel[3].astype(jnp.bfloat16), "seq", 1 - members).astype(jnp.float32),
            passed_along(travel[4].astype(jnp.bfloat16), "seq", 1 - members).astype(jnp.float32),
        )
        travel = jax.tree.map(
            lambda near_piece, far_piece: jnp.where(position == 0, far_piece, near_piece),
            onward,
            beside_all,
        )
        return (grad_queries + part_queries, travel)

    grad_queries, travel = lax.fori_loop(
        0, members, turn, (jnp.zeros(queries.shape, jnp.float32), travel)
    )
    return (grad_queries, travel[3], travel[4])


def attention_forward(queries, key_rows, value_rows, valid_tiles):
    local_heads = queries.shape[1]
    row_count = queries.shape[0]
    running = None
    for branch in range(BRANCHES):
        stride = 2**branch
        seg_width = SEGMENT * stride
        chosen = head_choice(stride, local_heads)
        selected = (
            pick(queries, chosen),
            pick(key_rows, chosen),
            pick(value_rows, chosen),
            pick(valid_tiles, chosen),
        )
        if seg_width <= row_count:
            result = local_forward(selected)
        else:
            result = relay_forward(selected, seg_width // row_count)
        branch_part = (
            spread(result[0], chosen, absent_top),
            spread(result[1], chosen, 0.0),
            spread(result[2], chosen, 0.0),
        )
        running = branch_part if running is None else merge_state(running, branch_part)
    return running


def attention_backward(
    queries, key_rows, value_rows, valid_tiles, grad_attn, delta, row_top, row_total
):
    local_heads = queries.shape[1]
    row_count = queries.shape[0]
    grad_queries = jnp.zeros(queries.shape, jnp.float32)
    grad_keys = jnp.zeros(queries.shape, jnp.float32)
    grad_values = jnp.zeros(queries.shape, jnp.float32)
    for branch in range(BRANCHES):
        stride = 2**branch
        seg_width = SEGMENT * stride
        chosen = head_choice(stride, local_heads)
        selected = tuple(
            (
                pick(entry, chosen)
                for entry in (
                    queries,
                    key_rows,
                    value_rows,
                    valid_tiles,
                    grad_attn,
                    delta,
                    row_top,
                    row_total,
                )
            )
        )
        if seg_width <= row_count:
            part_queries, part_keys, part_values = local_backward(selected)
        else:
            part_queries, part_keys, part_values = relay_backward(selected, seg_width // row_count)
        grad_queries = grad_queries + spread(part_queries, chosen, 0.0)
        grad_keys = grad_keys + spread(part_keys, chosen, 0.0)
        grad_values = grad_values + spread(part_values, chosen, 0.0)
    return (grad_queries, grad_keys, grad_values)


def body(
    tokens,
    cotangent,
    valid_tiles,
    gain_first,
    shift_first,
    w_project,
    bias_project,
    w_output,
    bias_output,
    gain_second,
    shift_second,
    w_expand,
    bias_expand,
    w_reduce,
    bias_reduce,
):
    local_heads = HEADS // lax.axis_size("heads")
    group_width = local_heads * HEAD_DIM
    row_count = tokens.shape[0]
    inputs = tokens.astype(jnp.float32)
    normed, undo_first = jax.vjp(norm_rows, inputs, gain_first, shift_first)
    normed_low = normed.astype(jnp.bfloat16)
    project = jnp.einsum("td,dce->tce", normed_low, w_project, preferred_element_type=jnp.float32)
    queries = (
        (project[:, 0] + bias_project[0])
        .astype(jnp.bfloat16)
        .reshape(row_count, local_heads, HEAD_DIM)
    )
    key_rows = project[:, 1].astype(jnp.bfloat16).reshape(row_count, local_heads, HEAD_DIM)
    value_rows = (
        (project[:, 2] + bias_project[1])
        .astype(jnp.bfloat16)
        .reshape(row_count, local_heads, HEAD_DIM)
    )
    row_top, row_total, weighted = attention_forward(queries, key_rows, value_rows, valid_tiles)
    attended = weighted / row_total[:, :, None]
    attended_low = attended.reshape(row_count, group_width).astype(jnp.bfloat16)
    branch_out = (
        lax.psum(
            jnp.dot(attended_low, w_output, preferred_element_type=jnp.float32).astype(
                jnp.bfloat16
            ),
            "heads",
        ).astype(jnp.float32)
        + bias_output
    )
    middle = inputs + branch_out
    normed_two, undo_second = jax.vjp(norm_rows, middle, gain_second, shift_second)
    normed_two_low = normed_two.astype(jnp.bfloat16)
    expand = jnp.dot(normed_two_low, w_expand, preferred_element_type=jnp.float32) + bias_expand
    active, undo_gelu = jax.vjp(gelu_tanh, expand)
    active_low = active.astype(jnp.bfloat16)
    reduced = (
        lax.psum(
            jnp.dot(active_low, w_reduce, preferred_element_type=jnp.float32).astype(jnp.bfloat16),
            "heads",
        ).astype(jnp.float32)
        + bias_reduce
    )
    layer_out = middle + reduced
    grad_bias_reduce = jnp.sum(cotangent, axis=0)
    cotangent_low = cotangent.astype(jnp.bfloat16)
    grad_w_reduce = jnp.einsum(
        "tf,td->fd", active_low, cotangent_low, preferred_element_type=jnp.float32
    )
    grad_active = jnp.einsum(
        "td,fd->tf", cotangent_low, w_reduce, preferred_element_type=jnp.float32
    )
    (grad_expand,) = undo_gelu(grad_active)
    grad_bias_expand = jnp.sum(grad_expand, axis=0)
    grad_expand_low = grad_expand.astype(jnp.bfloat16)
    grad_w_expand = jnp.einsum(
        "td,tf->df", normed_two_low, grad_expand_low, preferred_element_type=jnp.float32
    )
    grad_normed_two = lax.psum(
        jnp.einsum(
            "tf,df->td", grad_expand_low, w_expand, preferred_element_type=jnp.float32
        ).astype(jnp.bfloat16),
        "heads",
    ).astype(jnp.float32)
    grad_middle_part, grad_gain_second, grad_shift_second = undo_second(grad_normed_two)
    grad_middle = cotangent + grad_middle_part
    grad_bias_output = jnp.sum(grad_middle, axis=0)
    grad_middle_low = grad_middle.astype(jnp.bfloat16)
    grad_w_output = jnp.einsum(
        "te,td->ed", attended_low, grad_middle_low, preferred_element_type=jnp.float32
    )
    grad_attended = jnp.einsum(
        "td,ed->te", grad_middle_low, w_output, preferred_element_type=jnp.float32
    )
    grad_attended_low = grad_attended.astype(jnp.bfloat16).reshape(row_count, local_heads, HEAD_DIM)
    delta = jnp.sum(grad_attended_low.astype(jnp.float32) * attended, axis=-1)
    grad_queries, grad_keys, grad_values = attention_backward(
        queries, key_rows, value_rows, valid_tiles, grad_attended_low, delta, row_top, row_total
    )
    grad_queries = grad_queries.reshape(row_count, group_width)
    grad_keys = grad_keys.reshape(row_count, group_width)
    grad_values = grad_values.reshape(row_count, group_width)
    grad_bias_project = jnp.stack([jnp.sum(grad_queries, axis=0), jnp.sum(grad_values, axis=0)])
    grad_project = jnp.stack([grad_queries, grad_keys, grad_values], axis=1).astype(jnp.bfloat16)
    grad_w_project = jnp.einsum(
        "td,tce->dce", normed_low, grad_project, preferred_element_type=jnp.float32
    )
    grad_normed = lax.psum(
        jnp.einsum(
            "tce,dce->td", grad_project, w_project, preferred_element_type=jnp.float32
        ).astype(jnp.bfloat16),
        "heads",
    ).astype(jnp.float32)
    grad_inputs_part, grad_gain_first, grad_shift_first = undo_first(grad_normed)
    grad_tokens = grad_middle + grad_inputs_part
    summed = lax.psum(
        (
            grad_gain_first,
            grad_shift_first,
            grad_w_project,
            grad_bias_project,
            grad_w_output,
            grad_bias_output,
            grad_gain_second,
            grad_shift_second,
            grad_w_expand,
            grad_bias_expand,
            grad_w_reduce,
            grad_bias_reduce,
        ),
        "seq",
    )
    return (
        layer_out,
        grad_tokens,
        summed[0],
        summed[1],
        summed[2],
        summed[3],
        summed[4],
        summed[5],
        summed[6],
        summed[7],
        summed[8],
        summed[9],
        summed[10],
        summed[11],
    )


def solution(mesh):
    in_specs = (
        P("seq", None),
        P("seq", None),
        P("seq"),
        P(),
        P(),
        P(None, None, "heads"),
        P(None, "heads"),
        P("heads", None),
        P(),
        P(),
        P(),
        P(None, "heads"),
        P("heads"),
        P("heads", None),
        P(),
    )
    out_specs = (
        P("seq", None),
        P("seq", None),
        P(),
        P(),
        P(None, None, "heads"),
        P(None, "heads"),
        P("heads", None),
        P(),
        P(),
        P(),
        P(None, "heads"),
        P("heads"),
        P("heads", None),
        P(),
    )
    return jax.shard_map(body, mesh=mesh, in_specs=in_specs, out_specs=out_specs, check_vma=False)
```

profile of v0, /device:TPU:0, one launch (start us, length us, event | category | flops | bytes accessed | tf_op | source)
XLA Modules:
  0.0 2747.7 jit_solution(6903892326153126839)
XLA Ops:
  70.4 7.2 fusion.192
  83.0 7.4 fusion.188
  97.1 7.6 fusion.184
  119.6 316.7 %while.198 = (s32[]{:T(128)}, f32[64,8]{0,1:T(8,128)S(1)}, f32[64,8]{0,1:T(8,128)}, f32[64,8,48]{0,2,1:T(8,128)}, bf16[64,8,48]{0,2,1:T(8,128)(2,1)}, /*index=5*...) while((s32[]{:T(128)}, f32[64,8]{0,1:T(8,128)S(1)}, ...), condition=%wide.region_41.42_spmd, body=%wide.region_38.41_spmd.sunk | while | flops 6686722 | bytes 2269584 | solution.py:185
  436.9 162.7 %while.197 = (s32[]{:T(128)}, f32[128,8]{0,1:T(8,128)S(1)}, f32[128,8]{0,1:T(8,128)}, f32[128,8,48]{0,2,1:T(8,128)}, bf16[128,8,48]{0,2,1:T(8,128)(2,1)}, /*inde...) while((s32[]{:T(128)}, f32[128,8]{0,1:T(8,128)S(1)}, ...), condition=%wide.region_31.32_spmd, body=%wide.region_28.31_spmd.sunk | while | flops 26546176 | bytes 5325200 | solution.py:185
  496.0 5.4 collective-permute-done.8
  519.6 5.5 collective-permute-done.8
  541.2 7.2 collective-permute-done.8
  564.8 5.3 collective-permute-done.8
  600.2 76.9 %while.196 = (s32[]{:T(128)}, f32[256,8]{0,1:T(8,128)S(1)}, f32[256,8]{0,1:T(8,128)}, f32[256,8,48]{0,2,1:T(8,128)}, bf16[256,8,48]{0,2,1:T(8,128)(2,1)}, /*inde...) while((s32[]{:T(128)}, f32[256,8]{0,1:T(8,128)S(1)}, ...), condition=%wide.region_21.22_spmd, body=%wide.region_18.21_spmd.sunk | while | flops 106831872 | bytes 17007104 | solution.py:185
  615.0 5.6 collective-permute-done.2
  639.8 5.6 collective-permute-done.2
  665.5 5.6 collective-permute-done.2
  694.5 8.5 select_reduce_fusion.7
  716.0 56.0 %while.195 = (s32[]{:T(128)}, f32[8,1024,1]{1,0,2:T(8,128)S(1)}, f32[8,1024,1]{1,0,2:T(8,128)}, f32[8,1024,1,48]{1,3,2,0:T(8,128)}, s32[8,1024,1]{1,2,0:T(1,128)...) while((s32[]{:T(128)}, f32[8,1024,1]{1,0,2:T(8,128)S(1)}, ...), condition=%wide.region_5.6_spmd, body=%wide.region_2.5_spmd.sunk | while | flops 212915200 | bytes 13146233 | solution.py:144
  905.5 59.1 %all-reduce.8.cloned.1.call-done = bf16[1024,768]{1,0:T(8,128)(2,1)} async-done(((bf16[1024,768]{1,0:T(8,128)(2,1)}), bf16[1024,768]{1,0:T(8,128)(2,1)}) %all-reduce.8.cloned.1.call-update) | async-done | bytes 1572880 | tf_op jit(solution)/shard_map/psum | solution.py:336
  971.9 7.0 fusion.370
  1099.2 7.9 convolution_convert_fusion.2
  1167.4 93.5 %while.199 = (s32[]{:T(128)}, f32[8,1024,1,48]{1,3,2,0:T(8,128)}, f32[8,1024,1,48]{1,3,2,0:T(8,128)}, f32[8,1024,1,48]{1,3,2,0:T(8,128)}, bf16[8,1024,1,48]{1,3,...) while((s32[]{:T(128)}, f32[8,1024,1,48]{1,3,2,0:T(8,128)}, ...), condition=%wide.region_53.54_spmd, body=%wide.region_52.53_spmd.sunk | while | flops 512852992 | bytes 20201616 | solution.py:154
  1271.4 423.1 %while.203 = (s32[]{:T(128)}, f32[64,8,48]{0,2,1:T(8,128)S(1)}, bf16[64,8,48]{0,2,1:T(8,128)(2,1)S(1)}, bf16[64,8,48]{0,2,1:T(8,128)(2,1)S(1)}, s32[64,8]{0,1:T(...) while((s32[]{:T(128)}, f32[64,8,48]{0,2,1:T(8,128)S(1)}, ...), condition=%wide.region_77.78_spmd.clone, body=%wide.region_76.77_spmd.clone.sunk | while | flops 16466947 | bytes 3719214 | solution.py:227
  1310.5 5.8 collective-permute-done.55
  1336.5 6.0 collective-permute-done.55
  1362.9 6.0 collective-permute-done.55
  1389.2 6.0 collective-permute-done.55
  1415.5 6.0 collective-permute-done.55
  1441.8 6.0 collective-permute-done.55
  1468.1 6.0 collective-permute-done.55
  1494.4 6.0 collective-permute-done.55
  1520.7 6.0 collective-permute-done.55
  1547.0 6.0 collective-permute-done.55
  1573.3 6.0 collective-permute-done.55
  1599.6 6.0 collective-permute-done.55
  1625.9 6.0 collective-permute-done.55
  1652.2 6.0 collective-permute-done.55
  1678.5 6.0 collective-permute-done.55
  1699.8 271.8 %while.202 = (s32[]{:T(128)}, f32[128,8,48]{0,2,1:T(8,128)}, bf16[128,8,48]{0,2,1:T(8,128)(2,1)S(1)}, bf16[128,8,48]{0,2,1:T(8,128)(2,1)S(1)}, s32[128,8]{0,1:T(...) while((s32[]{:T(128)}, f32[128,8,48]{0,2,1:T(8,128)}, ...), condition=%wide.region_71.72_spmd.clone, body=%wide.region_70.71_spmd.clone.sunk | while | flops 64980992 | bytes 8617518 | solution.py:227
  1711.4 6.7 collective-permute-done.45
  1764.3 7.3 collective-permute-start.41
  1782.1 5.3 collective-permute-done.45
  1796.5 5.9 collective-permute-start.43
  1816.9 6.2 collective-permute-done.45
  1850.1 5.9 collective-permute-done.45
  1865.5 6.3 collective-permute-start.43
  1886.7 5.8 collective-permute-done.45
  1920.1 6.2 collective-permute-done.45
  1935.6 6.0 collective-permute-start.43
  1956.5 5.7 collective-permute-done.45
  1979.8 167.4 %while.201 = (s32[]{:T(128)}, f32[256,8,48]{0,2,1:T(8,128)}, bf16[256,8,48]{0,2,1:T(8,128)(2,1)S(1)}, bf16[256,8,48]{0,2,1:T(8,128)(2,1)}, s32[256,8]{0,1:T(8,12...) while((s32[]{:T(128)}, f32[256,8,48]{0,2,1:T(8,128)}, ...), condition=%wide.region_65.66_spmd.clone, body=%wide.region_64.65_spmd.clone.sunk | while | flops 258150400 | bytes 25885312 | solution.py:227
  2017.1 8.0 collective-permute-start.33
  2044.2 6.3 collective-permute-done.35
  2060.7 7.1 collective-permute-start.33
  2088.0 6.8 collective-permute-done.35
  2104.9 7.9 collective-permute-start.33
  2159.1 101.8 %while.200 = (s32[]{:T(128)}, f32[512,8,48]{0,2,1:T(8,128)S(1)}, bf16[512,8,48]{0,2,1:T(8,128)(2,1)S(1)}, bf16[512,8,48]{0,2,1:T(8,128)(2,1)}, s32[512,8]{0,1:T(...) while((s32[]{:T(128)}, f32[512,8,48]{0,2,1:T(8,128)S(1)}, ...), condition=%wide.region_59.60_spmd.clone, body=%wide.region_58.59_spmd.clone.sunk | while | flops 1029054464 | bytes 66007700 | solution.py:227
  2159.2 9.4 collective-permute-start.23
  2206.7 15.1 collective-permute-start.23
  2352.3 8.4 add_convert_fusion.11
  2366.9 7.7 fusion.223
  2374.6 9.5 fusion.258
  2420.8 7.4 fusion.222
  2428.4 34.8 %all-reduce.14.cloned.1.call-done = (bf16[1024,768]{1,0:T(8,128)(2,1)}, bf16[1024,768]{1,0:T(8,128)(2,1)}) async-done(((bf16[1024,768]{1,0:T(8,128)(2,1)}, bf16[1024,768]{1,0:T(8,128)(2,1)}), (bf16[1024,768]{1,0:T(8,128)(2,1)}, bf16[1024,768]{1,0:T(8,128)(2,1)})) %all-reduce.14.cloned.1.call-update) | async-done | bytes 3145744 | tf_op jit(solution)/shard_map/psum | solution.py:351
  2467.9 65.0 %all-reduce = (f32[768]{0:T(1024)}, f32[768]{0:T(1024)}, f32[2,384]{1,0:T(2,128)}, f32[768]{0:T(1024)}, f32[768]{0:T(1024)}, /*index=5*/f32[768]{0:T(1024)}, f32[1536]{0:T(1024)}, f32[768]{0:T(1024)}) all-reduce(f32[768]{0:T(1024)S(1)} %get-tuple-element.1568, ...), channel_id=1, replica_groups=mesh['seq'=16,'heads'=2] {'seq'}, use_global_device_ids=true, to_apply=%region_82.83 | all-reduce | flops 6912 | bytes 55296 | tf_op jit(solution)/shard_map/psum | solution.py:409
  2532.9 5.9 add_add_fusion.2
  2538.8 190.0 %all-reduce.12.cloned.1.call-done = (f32[768,3,384]{2,0,1:T(8,128)}, f32[384,768]{1,0:T(8,128)}, f32[768,1536]{1,0:T(8,128)}, f32[1536,768]{1,0:T(8,128)}) async-done(((f32[768,3,384]{2,0,1:T(8,128)}, f32[384,768]{1,0:T(8,128)}, f32[768,1536]{1,0:T(8,128)}, f32[1536,768]{1,0:T(8,128)}), (f32[768,3,384]{2,0,1:T(8,128)}, f32[384,768]{1,0:T(8,128)}, f32[768,1536]{1,0:T(8,128)}, ...) | async-done | bytes 14155792 | tf_op jit(solution)/shard_map/psum | solution.py:409
  (2599 shorter events, 2028.9 us)
Async XLA Ops:
  7.2 957.4 %all-reduce.8.cloned.1.call-start = ((), (), s32[]{:S(2)}) async-start(), calls=%async_computation | async-start | bytes 3145728 | tf_op jit(solution)/shard_map/psum | solution.py:336
  630.3 18.0 collective-permute-start.4
  656.0 18.0 collective-permute-start.4
  677.1 176.4 %collective-permute-start.59 = (s32[512,8]{1,0:T(8,128)}, s32[512,8]{1,0:T(8,128)}, u32[]{:S(2)}, u32[]{:S(2)}) collective-permute-start(s32[512,8]{1,0:T(8,128)} %copy.1035), channel_id=1, source_target_pairs={{0,2},{2,4},{4,6},{6,8},{8,10},{10,12},{12,14},{14,16},{16,18},{18... | collective-permute-start | bytes 49160 | tf_op jit(solution)/shard_map/while/body/eval_jaxpr/ppermute | solution.py:24
  681.6 173.3 %collective-permute-start.58 = (s32[512,8]{1,0:T(8,128)}, s32[512,8]{1,0:T(8,128)}, u32[]{:S(2)}, u32[]{:S(2)}) collective-permute-start(s32[512,8]{1,0:T(8,128)} %copy.1035), channel_id=1, source_target_pairs={{2,0},{4,2},{6,4},{8,6},{10,8},{12,10},{14,12},{16,14},{18,16},{20... | collective-permute-start | bytes 49160 | tf_op jit(solution)/shard_map/while/body/eval_jaxpr/ppermute | solution.py:24
  704.8 153.2 %collective-permute-start.61 = (bf16[512,8,48]{0,2,1:T(8,128)(2,1)S(1)}, bf16[512,8,48]{0,2,1:T(8,128)(2,1)}, u32[]{:S(2)}, u32[]{:S(2)}) collective-permute-start(bf16[512,8,48]{0,2,1:T(8,128)(2,1)S(1)} %copy.762), channel_id=1, source_target_pairs={{0,2},{2,4},{4,6},{6,8},{8,10},{10,12},{12,14},{14,16},{16,18},{18... | collective-permute-start | bytes 1179656 | tf_op jit(solution)/shard_map/while/body/eval_jaxpr/ppermute | solution.py:24
  709.8 148.2 %collective-permute-start.60 = (bf16[512,8,48]{0,2,1:T(8,128)(2,1)S(1)}, bf16[512,8,48]{0,2,1:T(8,128)(2,1)}, u32[]{:S(2)}, u32[]{:S(2)}) collective-permute-start(bf16[512,8,48]{0,2,1:T(8,128)(2,1)S(1)} %copy.762), channel_id=1, source_target_pairs={{2,0},{4,2},{6,4},{8,6},{10,8},{12,10},{14,12},{16,14},{18,16},{20... | collective-permute-start | bytes 1179656 | tf_op jit(solution)/shard_map/while/body/eval_jaxpr/ppermute | solution.py:24
  849.3 29.1 %collective-permute-start.63 = (bf16[512,8,48]{0,2,1:T(8,128)(2,1)S(1)}, bf16[512,8,48]{0,2,1:T(8,128)(2,1)}, u32[]{:S(2)}, u32[]{:S(2)}) collective-permute-start(bf16[512,8,48]{0,2,1:T(8,128)(2,1)S(1)} %copy.772), channel_id=1, source_target_pairs={{0,2},{2,4},{4,6},{6,8},{8,10},{10,12},{12,14},{14,16},{16,18},{18... | collective-permute-start | bytes 1179656 | tf_op jit(solution)/shard_map/while/body/eval_jaxpr/ppermute | solution.py:24
  853.6 24.8 collective-permute-start.62
  905.0 202.1 %all-reduce.10.cloned.1.call-start = ((), (), s32[]{:S(2)}) async-start(), calls=%async_computation.1 | async-start | bytes 3145728 | tf_op jit(solution)/shard_map/psum | solution.py:372
  984.3 1478.9 %all-reduce.14.cloned.1.call-start = ((), (), s32[]{:S(2)}) async-start(), calls=%async_computation.3 | async-start | bytes 6291456 | tf_op jit(solution)/shard_map/psum | solution.py:351
  1274.4 18.1 collective-permute-start.51
  1702.5 18.3 collective-permute-start.41
  1703.8 18.3 collective-permute-start.40
  1729.8 21.8 collective-permute-start.41
  1732.9 20.8 collective-permute-start.40
  1734.2 19.5 collective-permute-start.39
  1758.5 19.7 collective-permute-start.43
  1764.3 25.7 collective-permute-start.41
  1771.7 19.7 collective-permute-start.40
  1773.0 18.4 collective-permute-start.39
  1803.7 22.0 collective-permute-start.41
  1807.1 20.0 collective-permute-start.40
  1808.4 18.7 collective-permute-start.39
  1838.3 20.3 collective-permute-start.41
  1840.3 20.0 collective-permute-start.40
  1841.6 18.7 collective-permute-start.39
  1865.5 17.9 collective-permute-start.43
  1873.0 22.1 collective-permute-start.41
  1876.9 20.4 collective-permute-start.40
  1878.2 19.1 collective-permute-start.39
  1908.4 20.5 collective-permute-start.41
  1910.3 19.9 collective-permute-start.40
  1911.6 18.7 collective-permute-start.39
  1942.8 22.0 collective-permute-start.41
  1946.4 20.6 collective-permute-start.40
  1947.7 19.3 collective-permute-start.39
  1980.1 18.1 collective-permute-start.33
  1986.6 23.7 collective-permute-start.31
  1989.5 24.5 collective-permute-start.30
  1990.8 24.9 collective-permute-start.29
  2017.1 24.1 collective-permute-start.33
  2026.4 27.5 collective-permute-start.31
  2031.5 25.4 collective-permute-start.30
  2032.8 25.8 collective-permute-start.29
  2060.7 23.3 collective-permute-start.33
  2069.1 29.1 %collective-permute-start.31 = (bf16[256,8,48]{0,2,1:T(8,128)(2,1)}, bf16[256,8,48]{0,2,1:T(8,128)(2,1)}, u32[]{:S(2)}, u32[]{:S(2)}) collective-permute-start(bf16[256,8,48]{0,2,1:T(8,128)(2,1)} %get-tuple-element.2786), channel_id=1, source_target_pairs={{0,2},{2,4},{4,6},{6,8},{8,10},{10,12},{12,14},{14,16},{16,18},{18... | collective-permute-start | bytes 589832 | tf_op jit(solution)/shard_map/while/body/eval_jaxpr/ppermute | solution.py:24
  2074.3 26.4 collective-permute-start.30
  2075.5 26.8 collective-permute-start.29
  2104.9 23.2 collective-permute-start.33
  2114.1 26.3 collective-permute-start.31
  2118.4 25.5 collective-permute-start.30
  2119.7 25.8 collective-permute-start.29
  2159.2 31.2 %collective-permute-start.23 = (s32[512,8]{0,1:T(8,128)S(1)}, s32[512,8]{0,1:T(8,128)}, u32[]{:S(2)}, u32[]{:S(2)}) collective-permute-start(s32[512,8]{0,1:T(8,128)S(1)} %get-tuple-element.2871), channel_id=1, source_target_pairs={{0,2},{2,4},{4,6},{6,8},{8,10},{10,12},{12,14},{14,16},{16,18},{18... | collective-permute-start | bytes 49160 | tf_op jit(solution)/shard_map/while/body/eval_jaxpr/ppermute | solution.py:24
  2168.5 23.1 collective-permute-start.22
  2169.8 23.9 collective-permute-start.21
  2174.0 23.9 collective-permute-start.20
  2175.3 25.7 collective-permute-start.19
  2206.7 37.9 %collective-permute-start.23 = (s32[512,8]{0,1:T(8,128)S(1)}, s32[512,8]{0,1:T(8,128)}, u32[]{:S(2)}, u32[]{:S(2)}) collective-permute-start(s32[512,8]{0,1:T(8,128)S(1)} %get-tuple-element.2871), channel_id=1, source_target_pairs={{0,2},{2,4},{4,6},{6,8},{8,10},{10,12},{12,14},{14,16},{16,18},{18... | collective-permute-start | bytes 49160 | tf_op jit(solution)/shard_map/while/body/eval_jaxpr/ppermute | solution.py:24
  2221.8 24.1 collective-permute-start.22
  2223.1 24.9 collective-permute-start.21
  2228.3 23.9 collective-permute-start.20
  2229.6 25.7 collective-permute-start.19
  2365.6 363.2 %all-reduce.12.cloned.1.call-start = ((), (), s32[]{:S(2)}) async-start(), calls=%async_computation.2 | async-start | bytes 28311552 | tf_op jit(solution)/shard_map/psum | solution.py:409
  (731 other events, 7757.6 us)
Sparse Core Ops, SparseCore 0:
  905.2 59.3 all-reduce.7
  984.4 51.4 all-reduce.9
  2365.7 97.4 all-reduce.13
  2469.4 259.2 all-reduce.11
where the time goes:
time: 2780 us; the launch traced here: 2750 us
  starting transfers between devices  817 us (29%)
  waiting for transfers between devices  717 us (26%)
  local copies, waits for them, and re-layouts  522 us (19%)
  matrix products  342 us (12%)
  other arithmetic  257 us (9%)
  blocking collectives  65 us (2%)
    ppermute x456, starting transfers between devices, passed_along(): return lax.ppermute(value, axis, pairs)  816 us
    ppermute x456, waiting for transfers between devices, passed_along(): return lax.ppermute(value, axis, pairs)  433 us
    broadcast_in_dim x109, local copies, waits for them, and re-layouts, spread(): jnp.where(marker, branch_part[:, None], jnp.asarray(filler, branch_part.d...  262 us
    psum x1, waiting for transfers between devices, body(): lax.psum((grad_gain_first, grad_shift_first, grad_w_project, grad_bias_pr...  190 us
    dot_general x38, matrix products, attend_step(): jnp.einsum('hqk,khe->qhe', raised.astype(jnp.bfloat16), value_rows, prefe...  81.3 us
    select_n x200, other arithmetic, turn(): jnp.where(position == 0, far_piece, near_piece)  66.6 us
    psum x1, blocking collectives, body(): lax.psum((grad_gain_first, grad_shift_first, grad_w_project, grad_bias_pr...  65 us
    psum x1, waiting for transfers between devices, body(): lax.psum(jnp.dot(attended_low, w_output, preferred_element_type=jnp.float...  59.1 us
  transfers between devices with their start and end apart: 460, of which 124 were waited for; matrix products, arithmetic and copies ran while one was open for 21% of the time, Pallas kernels for 0%

commit v1 on v0

v1 whole, which is shorter than its diff:
```python
import functools
import math

import jax
import jax.numpy as jnp
from jax import lax
from jax.experimental import pallas as pl
from jax.experimental.pallas import tpu as pltpu
from jax.sharding import PartitionSpec as P

HEADS = 16
HEAD_DIM = 48
SEGMENT = 1024
BRANCHES = 5
LOCAL = 8

MESH = pl.DeviceIdType.MESH
BF = jnp.bfloat16
F32 = jnp.float32
NT = (((1,), (1,)), ((), ()))
TN = (((0,), (0,)), ((), ()))
NN = (((1,), (0,)), ((), ()))

masked_score = -1000000000.0
layer_eps = 1e-05
SCALE = HEAD_DIM ** (-0.5)
LOG2E = math.log2(math.e)


def dot(a, b, dims):
    return lax.dot_general(a, b, dims, preferred_element_type=F32)


def lanes(shape):
    return lax.broadcasted_iota(jnp.int32, shape, len(shape) - 1)


def reversed_bits(value, bits):
    out = value * 0
    for k in range(bits):
        out = out * 2 + (value // 2**k) % 2
    return out


def split3(value):
    high = value.astype(BF).astype(F32)
    rest = value - high
    middle = rest.astype(BF).astype(F32)
    return high, middle, rest - middle


class Place:
    def __init__(self):
        self.me = lax.axis_index("seq")
        self.y = lax.axis_index("heads")

    def member(self, b):
        return self.me % 2**b

    def device(self, b, j):
        return (self.me // 2**b * 2**b + j, self.y)

    def start(self, b, head):
        stride = 2**b
        place = (self.y * LOCAL + head) % stride
        return pl.multiple_of(reversed_bits(place, b) * (SEGMENT // stride), SEGMENT // stride)

    def greet(self):
        barrier = pltpu.get_barrier_semaphore()
        i = self.member(4)

        def signal(d, _):
            pl.semaphore_signal(barrier, inc=1, device_id=self.device(4, (i + d) % 16), device_id_type=MESH)
            return 0

        lax.fori_loop(1, 16, signal, 0)
        pl.semaphore_wait(barrier, 15)


def remote(src, dst, send, recv, device):
    return pltpu.make_async_remote_copy(
        src_ref=src, dst_ref=dst, send_sem=send, recv_sem=recv, device_id=device, device_id_type=MESH
    )


def over_peers(b, body):
    tiles = max(LOCAL // 2**b, 1)

    def step(d, _):
        for t in range(tiles):
            body(d, t)
        return 0

    lax.fori_loop(1, 2**b, step, 0)


def ds(start, size):
    return pl.ds(pl.multiple_of(start, size), size)


def attend(q, kv):
    scores = dot(q, kv, NT)
    top = jnp.max(scores, axis=1, keepdims=True)
    raised = jnp.exp2(scores - top).astype(BF)
    return dot(raised, kv, NN), top


def packed(out, top):
    lane = lanes(out.shape)
    total = out[:, 112:113]
    tile = jnp.where(lane == 112, 1.0, out * (1.0 / total))
    for k, piece in enumerate(split3(top) + split3(total)):
        tile = jnp.where(lane == 114 + k, piece, tile)
    return tile.astype(BF)


def forward_kernel(
    x_ref, fin_ref, att_ref, x1, x2, x3, q4, kv4, acc, tops, o1, o2, o3, o4, r1, r2, r3, r4, *sems
):
    place = Place()
    me = place.me
    xs, os, rs = (None, x1, x2, x3), (None, o1, o2, o3, o4), (None, r1, r2, r3, r4)
    go_send, go_recv, back_send, back_recv = sems[0:4], sems[4:8], sems[8:12], sems[12:16]

    def go(b, d, t):
        n, tiles = SEGMENT // 2**b, max(LOCAL // 2**b, 1)
        i = place.member(b)
        j = (i + d) % 2**b
        if b < 4:
            head = j * tiles + t
            k = (d - 1) * tiles + t
            return [
                remote(
                    x_ref.at[head, pl.ds(place.start(b, head), n), :],
                    xs[b].at[t, ds(i * n, n), :],
                    go_send[b - 1].at[k],
                    go_recv[b - 1].at[k],
                    place.device(b, j),
                )
            ]
        head, half = j // 2, j % 2
        start = place.start(4, head)
        k = (d - 1) * 2
        return [
            remote(
                x_ref.at[head, ds(start + half * 32, 32), 0:128],
                q4.at[ds(i * 32, 32), :],
                go_send[3].at[k],
                go_recv[3].at[k],
                place.device(4, j),
            ),
            remote(
                x_ref.at[head, pl.ds(start, 64), 128:256],
                kv4.at[ds(i * 64, 64), :],
                go_send[3].at[k + 1],
                go_recv[3].at[k + 1],
                place.device(4, j),
            ),
        ]

    def back(b, d, t):
        n, tiles = SEGMENT // 2**b, max(LOCAL // 2**b, 1)
        i = place.member(b)
        j = (i + d) % 2**b
        k = (d - 1) * tiles + t
        if b < 4:
            src, dst = o_at(b, t, j), rs[b].at[i * tiles + t]
        else:
            src, dst = o4.at[ds(j * 32, 32), :], r4.at[i // 2, ds(i % 2 * 32, 32), :]
        return remote(src, dst, back_send[b - 1].at[k], back_recv[b - 1].at[k], place.device(b, j))

    def o_at(b, t, j):
        n = SEGMENT // 2**b
        return os[b].at[t, ds(j * n, n), :]

    place.greet()
    for b in (4, 3, 2, 1):
        over_peers(b, lambda d, t: [c.start() for c in go(b, d, t)])

    for b in (1, 2, 3):
        n, tiles = SEGMENT // 2**b, LOCAL // 2**b
        i = place.member(b)
        for t in range(tiles):
            head = i * tiles + t
            xs[b][t, ds(i * n, n), :] = x_ref[head, pl.ds(place.start(b, head), n), :]
    i = place.member(4)
    start = place.start(4, i // 2)
    q4[ds(i * 32, 32), :] = x_ref[i // 2, ds(start + i % 2 * 32, 32), 0:128]
    kv4[ds(i * 64, 64), :] = x_ref[i // 2, pl.ds(start, 64), 128:256]

    def local_head(h, _):
        for half in range(2):
            rows = pl.ds(half * 512, 512)
            out, top = attend(x_ref[h, rows, 0:128], x_ref[h, :, 128:256])
            acc[h, rows, :] = out
            tops[h, rows, :] = jnp.broadcast_to(top, out.shape)
        return 0

    lax.fori_loop(0, 4, local_head, 0)

    over_peers(4, lambda d, t: [c.wait_recv() for c in go(4, d, t)])
    o4[...] = packed(*attend(q4[...], kv4[...]))
    over_peers(4, lambda d, t: back(4, d, t).start())
    r4[i // 2, ds(i % 2 * 32, 32), :] = o4[ds(i * 32, 32), :]
    for b in (3, 2, 1):
        n, tiles = SEGMENT // 2**b, LOCAL // 2**b
        over_peers(b, lambda d, t: [c.wait_recv() for c in go(b, d, t)])

        def tile(t, _):
            for half in range(2):
                rows = pl.ds(half * 512, 512)
                os[b][t, rows, :] = packed(*attend(xs[b][t, rows, 0:128], xs[b][t, :, 128:256]))
            return 0

        lax.fori_loop(0, tiles, tile, 0)
        over_peers(b, lambda d, t: back(b, d, t).start())
        j = place.member(b)
        for t in range(tiles):
            rs[b][j * tiles + t] = os[b][t, ds(j * n, n), :]

    lax.fori_loop(4, 8, local_head, 0)

    for b in (4, 3, 2, 1):
        over_peers(b, lambda d, t: back(b, d, t).wait_recv())

    row = lax.broadcasted_iota(jnp.int32, (128, 256), 0)
    column = lax.broadcasted_iota(jnp.int32, (128, 256), 1)
    first = jnp.where(column < 128, 114, 117)
    picks = jnp.where((row >= first) & (row < first + 3), 1.0, 0.0).astype(BF)

    def merge_head(h):
        for b in (1, 2, 3, 4):
            n = SEGMENT // 2**b
            rows = pl.ds(place.start(b, h), n)
            part = rs[b][h]
            stats = dot(part, picks, NN)
            top = jnp.maximum(tops[h, rows, :], stats[:, 0:128])
            keep = jnp.exp2(tops[h, rows, :] - top)
            gain = jnp.exp2(stats[:, 0:128] - top) * stats[:, 128:256]
            acc[h, rows, :] = acc[h, rows, :] * keep + part.astype(F32) * gain
            tops[h, rows, :] = top
        out = acc[h]
        lane = lanes(out.shape)
        inverse = 1.0 / out[:, 112:113]
        out = jnp.where((lane >= 64) & (lane < 112), out * inverse, 0.0)
        fin_ref[h] = jnp.where(lane == 112, inverse, jnp.where(lane == 113, tops[h], out))
        return out

    def pair(k, _):
        even, odd = merge_head(k * 2), merge_head(k * 2 + 1)
        att_ref[:, ds(k * 128, 128)] = (pltpu.roll(even, 64, 1) + odd).astype(BF)
        return 0

    lax.fori_loop(0, LOCAL // 2, pair, 0)

    for b in (4, 3, 2, 1):
        over_peers(b, lambda d, t: [c.wait_send() for c in go(b, d, t)])
        over_peers(b, lambda d, t: back(b, d, t).wait_send())


def sem_shapes(per_copy):
    counts = [4, 6, 7, 15 * per_copy]
    return [pltpu.SemaphoreType.DMA((c,)) for c in counts]


VMEM = pl.BlockSpec(memory_space=pltpu.VMEM)


def attention_forward(x):
    shapes = [
        ((LOCAL, SEGMENT, 128), F32),
        ((SEGMENT, LOCAL * 64), BF),
        ((4, SEGMENT, 256), BF),
        ((2, SEGMENT, 256), BF),
        ((1, SEGMENT, 256), BF),
        ((512, 128), BF),
        ((SEGMENT, 128), BF),
    ]
    scratch = [
        ((LOCAL, SEGMENT, 128), F32),
        ((LOCAL, SEGMENT, 128), F32),
        ((4, SEGMENT, 128), BF),
        ((2, SEGMENT, 128), BF),
        ((1, SEGMENT, 128), BF),
        ((512, 128), BF),
        ((LOCAL, 512, 128), BF),
        ((LOCAL, 256, 128), BF),
        ((LOCAL, 128, 128), BF),
        ((LOCAL, 64, 128), BF),
    ]
    return pl.pallas_call(
        forward_kernel,
        out_shape=[jax.ShapeDtypeStruct(*s) for s in shapes],
        in_specs=[VMEM],
        out_specs=[VMEM] * len(shapes),
        scratch_shapes=[pltpu.VMEM(*s) for s in scratch]
        + sem_shapes(2) + sem_shapes(2) + sem_shapes(1) + sem_shapes(1),
        compiler_params=pltpu.CompilerParams(
            collective_id=0, has_side_effects=True, vmem_limit_bytes=56 * 2**20
        ),
        name="attention_forward",
    )(x)


def pair_grads(q, d, kv_at, put):
    lane = lanes(q.shape)
    zero = jnp.zeros_like(d)
    queries = q + jnp.where(lane < 64, d, zero)
    grads = jnp.where(lane < 64, zero, d)
    total = None
    for half in range(2):
        kv = kv_at(half)
        probs = jnp.exp2(dot(kv, queries, NT))
        grad_scores = (probs * dot(kv, grads, NT)).astype(BF)
        put(half, dot(grad_scores, queries, NN) + dot(probs.astype(BF), grads, NN))
        part = dot(kv, grad_scores, TN)
        total = part if total is None else total + part
    return total.T


def backward_kernel(
    x_ref, x1, x2, x3, q4, kv4, fin_ref, do_ref, g_ref, sum_ref,
    d0, d1, d2, d3, d4, total, g1, g2, g3, gq4, gkv4, r1, r2, r3, rq4, rkv4, *sems
):
    place = Place()
    me = place.me
    xs, dd, gs, rs = (None, x1, x2, x3), (None, d1, d2, d3), (None, g1, g2, g3), (None, r1, r2, r3)
    go_send, go_recv, back_send, back_recv = sems[0:4], sems[4:8], sems[8:12], sems[12:16]

    def go(b, d, t):
        n, tiles = SEGMENT // 2**b, max(LOCAL // 2**b, 1)
        i = place.member(b)
        j = (i + d) % 2**b
        k = (d - 1) * tiles + t
        if b < 4:
            head = j * tiles + t
            src, dst = d0.at[head, pl.ds(place.start(b, head), n), :], dd[b].at[t, ds(i * n, n), :]
        else:
            start = place.start(4, j // 2)
            src, dst = d0.at[j // 2, ds(start + j % 2 * 32, 32), :], d4.at[ds(i * 32, 32), :]
        return remote(src, dst, go_send[b - 1].at[k], go_recv[b - 1].at[k], place.device(b, j))

    def back(b, d, t):
        n, tiles = SEGMENT // 2**b, max(LOCAL // 2**b, 1)
        i = place.member(b)
        j = (i + d) % 2**b
        device = place.device(b, j)
        if b < 4:
            k = (d - 1) * tiles + t
            return [
                remote(
                    gs[b].at[t, ds(j * n, n), :],
                    rs[b].at[i * tiles + t],
                    back_send[b - 1].at[k],
                    back_recv[b - 1].at[k],
                    device,
                )
            ]
        k = (d - 1) * 2
        return [
            remote(
                gq4.at[ds(j * 32, 32), :],
                rq4.at[i // 2, ds(i % 2 * 32, 32), :],
                back_send[3].at[k],
                back_recv[3].at[k],
                device,
            ),
            remote(
                gkv4.at[ds(j * 64, 64), :],
                rkv4.at[i % 2, i // 2],
                back_send[3].at[k + 1],
                back_recv[3].at[k + 1],
                device,
            ),
        ]

    def prepare(h, _):
        fin = fin_ref[h]
        lane = lanes(fin.shape)
        value_lane = (lane >= 64) & (lane < 112)
        grad = (do_ref[:, ds(h * 128, 128)].astype(F32) * fin[:, 112:113]).astype(BF).astype(F32)
        delta = jnp.sum(jnp.where(value_lane, grad * fin, 0.0), axis=1, keepdims=True)
        tile = jnp.where(value_lane, grad, 0.0)
        high, middle, low = split3(-delta)
        tile = jnp.where(lane == 112, high, jnp.where(lane == 113, middle, tile))
        for k, piece in enumerate(split3(-fin[:, 113:114])):
            tile = jnp.where(lane == 52 + k, piece, tile)
        d0[h] = tile.astype(BF)
        return 0

    lax.fori_loop(0, LOCAL, prepare, 0)
    place.greet()
    for b in (4, 3, 2, 1):
        over_peers(b, lambda d, t: go(b, d, t).start())
    for b in (1, 2, 3):
        n, tiles = SEGMENT // 2**b, LOCAL // 2**b
        i = place.member(b)
        for t in range(tiles):
            head = i * tiles + t
            dd[b][t, ds(i * n, n), :] = d0[head, pl.ds(place.start(b, head), n), :]
    i = place.member(4)
    d4[ds(i * 32, 32), :] = d0[i // 2, ds(place.start(4, i // 2) + i % 2 * 32, 32), :]

    def local_head(h, _):
        def put(half, grad):
            total[h, pl.ds(half * 512, 512), 128:256] = grad

        total[h, :, 0:128] = pair_grads(
            x_ref[h, :, 0:128], d0[h], lambda half: x_ref[h, pl.ds(half * 512, 512), 128:256], put
        )
        return 0

    lax.fori_loop(0, 4, local_head, 0)

    over_peers(4, lambda d, t: go(4, d, t).wait_recv())

    def put4(half, grad):
        gkv4[pl.ds(half * 512, 512), :] = grad.astype(BF)

    gq4[...] = pair_grads(q4[...], d4[...], lambda half: kv4[pl.ds(half * 512, 512), :], put4).astype(BF)
    over_peers(4, lambda d, t: [c.start() for c in back(4, d, t)])
    rq4[i // 2, ds(i % 2 * 32, 32), :] = gq4[ds(i * 32, 32), :]
    rkv4[i % 2, i // 2] = gkv4[ds(i * 64, 64), :]
    for b in (3, 2, 1):
        n, tiles = SEGMENT // 2**b, LOCAL // 2**b
        over_peers(b, lambda d, t: go(b, d, t).wait_recv())

        def tile(t, _):
            def put(half, grad):
                gs[b][t, pl.ds(half * 512, 512), 128:256] = grad.astype(BF)

            gs[b][t, :, 0:128] = pair_grads(
                xs[b][t, :, 0:128], dd[b][t], lambda half: xs[b][t, pl.ds(half * 512, 512), 128:256], put
            ).astype(BF)
            return 0

        lax.fori_loop(0, tiles, tile, 0)
        over_peers(b, lambda d, t: [c.start() for c in back(b, d, t)])
        j = place.member(b)
        for t in range(tiles):
            rs[b][j * tiles + t] = gs[b][t, ds(j * n, n), :]

    lax.fori_loop(4, 8, local_head, 0)

    for b in (4, 3, 2, 1):
        over_peers(b, lambda d, t: [c.wait_recv() for c in back(b, d, t)])

    def finish(h, _):
        for b in (1, 2, 3):
            n = SEGMENT // 2**b
            rows = pl.ds(place.start(b, h), n)
            total[h, rows, :] += rs[b][h].astype(F32)
        rows = pl.ds(place.start(4, h), 64)
        total[h, rows, 0:128] += rq4[h].astype(F32)
        total[h, rows, 128:256] += rkv4[0, h].astype(F32) + rkv4[1, h].astype(F32)
        grad = total[h]
        lane = lanes(grad.shape)
        live = (x_ref[h, :, 176:177].astype(F32) >= 0.0).astype(F32)
        key_factor = live * (1.0 / LOG2E)
        grad = jnp.where(
            lane < 48,
            grad * SCALE,
            jnp.where(
                (lane >= 128) & (lane < 176),
                grad * key_factor,
                jnp.where((lane >= 192) & (lane < 240), grad, 0.0),
            ),
        )
        g_ref[h] = grad.astype(BF)
        sum_ref[h] = jnp.broadcast_to(jnp.sum(grad, axis=0, keepdims=True), (8, 256))
        return 0

    lax.fori_loop(0, LOCAL, finish, 0)

    for b in (4, 3, 2, 1):
        over_peers(b, lambda d, t: go(b, d, t).wait_send())
        over_peers(b, lambda d, t: [c.wait_send() for c in back(b, d, t)])


def attention_backward(x, saved, fin, grad_out):
    shapes = [((LOCAL, SEGMENT, 256), BF), ((LOCAL, 8, 256), F32)]
    scratch = [
        ((LOCAL, SEGMENT, 128), BF),
        ((4, SEGMENT, 128), BF),
        ((2, SEGMENT, 128), BF),
        ((1, SEGMENT, 128), BF),
        ((512, 128), BF),
        ((LOCAL, SEGMENT, 256), F32),
        ((4, SEGMENT, 256), BF),
        ((2, SEGMENT, 256), BF),
        ((1, SEGMENT, 256), BF),
        ((512, 128), BF),
        ((SEGMENT, 128), BF),
        ((LOCAL, 512, 256), BF),
        ((LOCAL, 256, 256), BF),
        ((LOCAL, 128, 256), BF),
        ((LOCAL, 64, 128), BF),
        ((2, LOCAL, 64, 128), BF),
    ]
    return pl.pallas_call(
        backward_kernel,
        out_shape=[jax.ShapeDtypeStruct(*s) for s in shapes],
        in_specs=[VMEM] * 8,
        out_specs=[VMEM] * len(shapes),
        scratch_shapes=[pltpu.VMEM(*s) for s in scratch]
        + sem_shapes(1) + sem_shapes(1) + sem_shapes(2) + sem_shapes(2),
        compiler_params=pltpu.CompilerParams(
            collective_id=1, has_side_effects=True, vmem_limit_bytes=60 * 2**20
        ),
        name="attention_backward",
    )(x, *saved, fin, grad_out)


def norm_rows(values, gain, shift):
    mean_row = jnp.mean(values, axis=-1, keepdims=True)
    centered = values - mean_row
    variance = jnp.mean(centered * centered, axis=-1, keepdims=True)
    return centered * lax.rsqrt(variance + layer_eps) * gain + shift


def gelu_tanh(values):
    return jax.nn.gelu(values, approximate=True)


ORDER = tuple(int(f"{c:04b}"[::-1], 2) for c in range(16))


def by_residue(rows):
    shaped = rows.reshape((rows.shape[0] // 16, 2, 2, 2, 2) + rows.shape[1:])
    rest = tuple(range(5, shaped.ndim))
    return shaped.transpose((4, 3, 2, 1, 0) + rest).reshape(rows.shape)


def from_residue(rows):
    shaped = rows.reshape((2, 2, 2, 2, rows.shape[0] // 16) + rows.shape[1:])
    rest = tuple(range(5, shaped.ndim))
    return shaped.transpose((4, 3, 2, 1, 0) + rest).reshape(rows.shape)


def wide(q, k, v):
    pad = lambda a, n: jnp.pad(a, [(0, 0)] * (a.ndim - 1) + [(0, n)])
    return jnp.concatenate([pad(q, 80), pad(k, 16), pad(v, 16)], axis=-1)


def body(
    tokens,
    cotangent,
    valid_tiles,
    gain_first,
    shift_first,
    w_project,
    bias_project,
    w_output,
    bias_output,
    gain_second,
    shift_second,
    w_expand,
    bias_expand,
    w_reduce,
    bias_reduce,
):
    rows = tokens.shape[0]
    width = tokens.shape[1]
    tokens = by_residue(tokens)
    cotangent = by_residue(cotangent)
    valid = by_residue(valid_tiles).astype(F32)
    inputs = tokens.astype(F32)
    normed, undo_first = jax.vjp(norm_rows, inputs, gain_first, shift_first)
    normed_low = normed.astype(BF)

    w_heads = w_project.reshape(width, 3, LOCAL, HEAD_DIM)
    w_wide = wide(w_heads[:, 0], w_heads[:, 1], w_heads[:, 2])
    b_heads = bias_project.reshape(2, LOCAL, HEAD_DIM)
    b_wide = wide(b_heads[0], jnp.zeros_like(b_heads[0]), b_heads[1])
    lane = jnp.arange(256)
    ones = (lane == 48) | ((lane >= 180) & (lane < 183)) | (lane == 240) | (lane == 241)
    x = jnp.einsum("td,dhe->hte", normed_low, w_wide, preferred_element_type=F32) + b_wide[:, None]
    x = jnp.where(lane < 48, x * (SCALE * LOG2E), x)
    x = jnp.where((lane >= 128) & (lane < 176), x * valid[:, None], x)
    x = jnp.where(ones, 1.0, jnp.where(lane == 176, ((1.0 - valid) * masked_score)[:, None], x)).astype(BF)

    fin, attended, *saved = attention_forward(x)

    w_out_rows = jnp.pad(w_output.reshape(LOCAL, HEAD_DIM, width), ((0, 0), (0, 16), (0, 0))).reshape(-1, width)
    w_out_wide = jnp.pad(w_output.reshape(LOCAL, HEAD_DIM, width), ((0, 0), (64, 16), (0, 0))).reshape(-1, width)
    branch_out = (
        lax.psum(jnp.dot(attended, w_out_rows, preferred_element_type=F32).astype(BF), "heads").astype(F32)
        + bias_output
    )
    middle = inputs + branch_out
    normed_two, undo_second = jax.vjp(norm_rows, middle, gain_second, shift_second)
    normed_two_low = normed_two.astype(BF)
    expand = jnp.dot(normed_two_low, w_expand, preferred_element_type=F32) + bias_expand
    active, undo_gelu = jax.vjp(gelu_tanh, expand)
    active_low = active.astype(BF)
    reduced = (
        lax.psum(jnp.dot(active_low, w_reduce, preferred_element_type=F32).astype(BF), "heads").astype(F32)
        + bias_reduce
    )
    layer_out = middle + reduced
    grad_bias_reduce = jnp.sum(cotangent, axis=0)
    cotangent_low = cotangent.astype(BF)
    grad_w_reduce = jnp.einsum("tf,td->fd", active_low, cotangent_low, preferred_element_type=F32)
    grad_active = jnp.einsum("td,fd->tf", cotangent_low, w_reduce, preferred_element_type=F32)
    (grad_expand,) = undo_gelu(grad_active)
    grad_bias_expand = jnp.sum(grad_expand, axis=0)
    grad_expand_low = grad_expand.astype(BF)
    grad_w_expand = jnp.einsum("td,tf->df", normed_two_low, grad_expand_low, preferred_element_type=F32)
    grad_normed_two = lax.psum(
        jnp.einsum("tf,df->td", grad_expand_low, w_expand, preferred_element_type=F32).astype(BF), "heads"
    ).astype(F32)
    grad_middle_part, grad_gain_second, grad_shift_second = undo_second(grad_normed_two)
    grad_middle = cotangent + grad_middle_part
    grad_bias_output = jnp.sum(grad_middle, axis=0)
    grad_middle_low = grad_middle.astype(BF)
    grad_w_output = (
        jnp.einsum("te,td->ed", attended, grad_middle_low, preferred_element_type=F32)
        .reshape(LOCAL, 64, width)[:, :HEAD_DIM]
        .reshape(-1, width)
    )
    grad_attended = jnp.einsum("td,ed->te", grad_middle_low, w_out_wide, preferred_element_type=F32).astype(BF)
    early = lax.psum(
        (grad_w_output.astype(BF), grad_w_expand.astype(BF), grad_w_reduce.astype(BF)), "seq"
    )

    g, g_sums = attention_backward(x, saved, fin, grad_attended)
    g_sums = g_sums[:, 0]
    grad_bias_project = jnp.stack([g_sums[:, 0:48].reshape(-1), g_sums[:, 192:240].reshape(-1)])
    grad_w_wide = jnp.einsum("td,hte->dhe", normed_low, g, preferred_element_type=F32)
    grad_w_project = jnp.stack(
        [grad_w_wide[:, :, k : k + 48].reshape(width, -1) for k in (0, 128, 192)], axis=1
    )
    grad_normed = lax.psum(
        jnp.einsum("hte,dhe->td", g, w_wide, preferred_element_type=F32).astype(BF), "heads"
    ).astype(F32)
    grad_inputs_part, grad_gain_first, grad_shift_first = undo_first(grad_normed)
    grad_tokens = grad_middle + grad_inputs_part
    grad_w_project = lax.psum(grad_w_project.astype(BF), "seq")
    summed = lax.psum(
        (
            grad_gain_first,
            grad_shift_first,
            grad_bias_project,
            grad_bias_output,
            grad_gain_second,
            grad_shift_second,
            grad_bias_expand,
            grad_bias_reduce,
        ),
        "seq",
    )
    return (
        from_residue(layer_out),
        from_residue(grad_tokens),
        summed[0],
        summed[1],
        grad_w_project.astype(F32),
        summed[2],
        early[0].astype(F32),
        summed[3],
        summed[4],
        summed[5],
        early[1].astype(F32),
        summed[6],
        early[2].astype(F32),
        summed[7],
    )


def solution(mesh):
    in_specs = (
        P("seq", None),
        P("seq", None),
        P("seq"),
        P(),
        P(),
        P(None, None, "heads"),
        P(None, "heads"),
        P("heads", None),
        P(),
        P(),
        P(),
        P(None, "heads"),
        P("heads"),
        P("heads", None),
        P(),
    )
    out_specs = (
        P("seq", None),
        P("seq", None),
        P(),
        P(),
        P(None, None, "heads"),
        P(None, "heads"),
        P("heads", None),
        P(),
        P(),
        P(),
        P(None, "heads"),
        P("heads"),
        P("heads", None),
        P(),
    )
    return jax.shard_map(body, mesh=mesh, in_specs=in_specs, out_specs=out_specs, check_vma=False)
```

time: 2780 us -> 589 us (0.21)
  starting transfers between devices: 817 us -> 0.57 us
  waiting for transfers between devices: 717 us -> 205 us
  local copies, waits for them, and re-layouts: 522 us -> 57.8 us
  matrix products: 342 us -> 64.2 us
  other arithmetic: 257 us -> 50.3 us
  Pallas kernels: 0 us -> 124 us
    ppermute x456 -> x0, starting transfers between devices: 816 us -> none  [passed_along(): return lax.ppermute(value, axis, pairs)]
    ppermute x456 -> x0, waiting for transfers between devices: 433 us -> none  [passed_along(): return lax.ppermute(value, axis, pairs)]
    broadcast_in_dim x125 -> x1, local copies, waits for them, and re-layouts: 283 us -> 0.01 us  [body(): b_wide = wide(b_heads[0], jnp.zeros_like(b_heads[0]), b_heads[1])]
    dot_general x275 -> x9, matrix products: 321 us -> 43.8 us  [the longest x1 7.95 us: body(): jnp.dot(active_low, w_reduce, preferred_element_type=F32).astype(BF)]
    pallas_call x0 -> x2, Pallas kernels: none -> 124 us  [the longest x1 65.7 us: attention_backward(): pl.pallas_call(backward_kernel, out_shape=[jax.ShapeDtypeStruct(*s) for s...]
    psum x3, waiting for transfers between devices: 284 us -> 163 us  [the longest x1 65.5 us: body(): grad_w_project = lax.psum(grad_w_project.astype(BF), 'seq')]
    reduce_sum x56 -> x1, other arithmetic: 77.1 us -> 2.13 us  [body(): grad_bias_reduce = jnp.sum(cotangent, axis=0)]
    select_n x202 -> x0, other arithmetic: 66.7 us -> none  [the longest x200 66.6 us: turn(): jnp.where(position == 0, far_piece, near_piece)]
  transfers between devices with their start and end apart: 460 -> 4, of which waited for: 124 -> 4; matrix products, arithmetic and copies ran while one was open for 21% -> 13% of each run, Pallas kernels for 0% -> 0%
where the time goes in v1:
time: 589 us; the launch traced here: 580 us
  waiting for transfers between devices  205 us (35%)
  Pallas kernels  124 us (21%)
  matrix products  64.2 us (11%)
  blocking collectives  63.7 us (11%)
  local copies, waits for them, and re-layouts  57.8 us (10%)
  other arithmetic  50.3 us (9%)
  between operations  14.5 us (2%)
    pallas_call x1, Pallas kernels, attention_backward(): pl.pallas_call(backward_kernel, out_shape=[jax.ShapeDtypeStruct(*s) for s...  65.7 us
    psum x1, waiting for transfers between devices, body(): grad_w_project = lax.psum(grad_w_project.astype(BF), 'seq')  65.5 us
    psum x1, blocking collectives, body(): lax.psum((grad_gain_first, grad_shift_first, grad_bias_project, grad_bias...  63.7 us
    pallas_call x1, Pallas kernels, attention_forward(): pl.pallas_call(forward_kernel, out_shape=[jax.ShapeDtypeStruct(*s) for s...  57.9 us
    psum x1, waiting for transfers between devices, body(): lax.psum(jnp.dot(active_low, w_reduce, preferred_element_type=F32).astype...  53.1 us
    psum x1, waiting for transfers between devices, body(): lax.psum(jnp.dot(attended, w_out_rows, preferred_element_type=F32).astype...  44.3 us
    psum x1, waiting for transfers between devices, body(): lax.psum(jnp.einsum('tf,df->td', grad_expand_low, w_expand, preferred_ele...  42.3 us
    unnamed x102, local copies, waits for them, and re-layouts  12.1 us
  transfers between devices with their start and end apart: 4, of which 4 were waited for; matrix products, arithmetic and copies ran while one was open for 13% of the time, Pallas kernels for 0%

profile of v1, /device:TPU:0, one launch (start us, length us, event | category | flops | bytes accessed | tf_op | source)
XLA Modules:
  0.0 579.9 jit_solution(2970834402612520453)
XLA Ops:
  8.3 4.9 reshape.187
  13.1 3.6 bitcast_reduce_fusion
  16.8 4.4 fusion.24
  21.3 3.5 copy.40
  24.8 0.6 and_select_fusion
  25.4 0.7 squeeze.21
  26.0 0.7 squeeze.22
  27.4 0.6 subtract_multiply_fusion
  28.0 3.8 copy.42
  31.9 2.4 slice_bitcast_fusion.2
  34.2 0.7 multiply_add_fusion
  34.9 0.8 add.142
  35.7 0.9 select_maximum_fusion
  36.5 2.4 add_convert_fusion.1
  39.0 1.1 copy-done.17
  40.1 6.4 %fusion.2.x_ref = bf16[8,1024,256]{2,1,0:T(8,128)(2,1)} fusion(f32[1024]{0:T(1024)} %copy-done.35, f32[8,256]{1,0:T(8,128)S(1)} %select_maximum_fusion, bf16[1024]{0:T(1024)(128)(2,1)} %subtract_multiply_fusion, pred[256]{0:T(512)(128)(4,1)} %get-tuple-element.72, pred[256]{0:T(512)(128)(4,1)} %get-tuple-element.71, pred[256]{0:T(512)(128)(4,1)} %get-tuple-element.73, ...), kind=kOutput, calls=%fused_computation.8 | convolution fusion | flops 3257925632 | bytes 7552000 | tf_op jit(solution)/shard_map/td,dhe->hte/dot_general | solution.py:577
  46.6 57.9 %attention_forward.1 = (f32[8,1024,128]{2,1,0:T(8,128)}, bf16[1024,512]{1,0:T(8,128)(2,1)}, bf16[4,1024,256]{2,1,0:T(8,128)(2,1)}, bf16[2,1024,256]{2,1,0:T(8,12...) custom-call(bf16[8,1024,256]{2,1,0:T(8,128)(2,1)} %fusion.2.x_ref), custom_call_target="tpu_custom_call" | custom-call | tf_op jit(solution)/shard_map/attention_forward/pallas_call | solution.py:291
  104.5 3.4 convolution_convert_fusion.4
  107.9 5.1 reshape.179
  113.1 3.7 copy.45
  116.8 1.7 copy-done.6
  118.4 1.3 bitcast_convert_fusion.1
  119.8 44.3 %all-reduce.16.cloned.1.call-done = bf16[1024,768]{1,0:T(8,128)(2,1)} async-done(((bf16[1024,768]{1,0:T(8,128)(2,1)}), bf16[1024,768]{1,0:T(8,128)(2,1)}) %all-reduce.16.cloned.1.call-update) | async-done | bytes 1572880 | tf_op jit(solution)/shard_map/psum | solution.py:587
  164.0 2.8 fusion.44
  167.5 0.6 copy-done.30
  168.6 0.6 copy-done.28
  169.2 0.6 copy-done.42
  169.7 2.8 fusion.40
  172.6 7.4 %fusion.41 = (f32[1536]{0:T(1024)}, bf16[1024,1536]{1,0:T(8,128)(2,1)S(1)}) fusion(f32[1024,1536]{1,0:T(8,128)S(1)} %fusion.40, f32[1536]{0:T(1024)S(1)} %copy-done.44, bf16[1024,768]{1,0:T(8,128)(2,1)S(1)} %copy-done.19, bf16[1536,768]{1,0:T(8,128)(2,1)S(1)} %copy-done), kind=kOutput, calls=%fused_computation.106 | convolution fusion | flops 2450520576 | bytes 13381632 | tf_op jit(solution)/shard_map/td,fd->tf/dot_general | solution.py:604
  180.0 1.7 copy-done.49
  181.7 3.7 convolution_convert_fusion.5
  185.4 1.4 pad.40
  186.8 7.9 %convolution_convert_fusion.6 = bf16[1024,768]{1,0:T(8,128)(2,1)} fusion(bf16[1536,768]{1,0:T(8,128)(2,1)S(1)} %copy-done, f32[1024,1536]{1,0:T(8,128)} %copy-done.48, f32[1536]{0:T(1024)} %param.27), kind=kOutput, calls=%fused_computation.61 | convolution fusion | flops 2432434176 | bytes 10229760 | tf_op jit(solution)/shard_map/dot_general | solution.py:597
  194.7 42.3 %all-reduce.18.cloned.1.call-done = bf16[1024,768]{1,0:T(8,128)(2,1)} async-done(((bf16[1024,768]{1,0:T(8,128)(2,1)}), bf16[1024,768]{1,0:T(8,128)(2,1)}) %all-reduce.18.cloned.1.call-update) | async-done | bytes 1572880 | tf_op jit(solution)/shard_map/psum | solution.py:609
  237.0 3.5 convert_reduce_fusion.1
  240.8 2.0 fusion.19
  242.9 1.6 fusion.43
  244.5 3.1 convolution_convert_fusion.3.do_ref
  247.7 65.7 %attention_backward.1 = (bf16[8,1024,256]{2,1,0:T(8,128)(2,1)}, f32[8,8,256]{2,1,0:T(8,128)}) custom-call(bf16[8,1024,256]{2,1,0:T(8,128)(2,1)} %fusion.2.x_ref, bf16[4,1024,256]{2,1,0:T(8,128)(2,1)} %get-tuple-element.24.x1, bf16[2,1024,256]{2,1,0:T(8,128)(2,1)} %get-tuple-element.25.x2, bf16[1,1024,256]{2,1,0:T(8,128)(2,1)} %get-tuple-element.26.x3, ...), custom_call_target="tpu_custom_call" | custom-call | tf_op jit(solution)/shard_map/attention_backward/pallas_call | solution.py:500
  313.4 7.8 %bitcast_convert_fusion = bf16[1024,768]{1,0:T(8,128)(2,1)} fusion(bf16[8,1024,256]{2,1,0:T(8,128)(2,1)} %get-tuple-element.30, bf16[768,8,48]{0,2,1:T(8,128)(2,1)S(1)} %copy-done.22, bf16[768,8,48]{0,2,1:T(8,128)(2,1)S(1)} %copy-done.24, bf16[768,8,48]{0,2,1:T(8,128)(2,1)S(1)} %get-tuple-element.65), kind=kOutput, calls=%fused_computation.42 | convolution fusion | flops 3244032000 | bytes 7536640 | tf_op jit(solution)/shard_map/hte,dhe->td/dot_general | solution.py:634
  321.9 8.3 %convolution_convert_fusion.1 = bf16[768,1536]{1,0:T(8,128)(2,1)} fusion(bf16[1024,1536]{1,0:T(8,128)(2,1)} %copy-done.49, f32[1024,768]{1,0:T(8,128)} %copy-done.3, f32[768]{0:T(1024)S(1)} %copy-done.47, f32[768]{0:T(1024)S(1)} %copy-done.27, f32[1024]{0:T(1024)S(1)} %copy-done.29, f32[1024]{0:T(1024)S(1)} %broadcast_multiply_fusion.1), kind=kOutput, calls=%fused_computation.35 | convolution fusion | flops 2421030912 | bytes 8665088 | tf_op jit(solution)/shard_map/td,tf->df/dot_general | solution.py:608
  330.2 8.4 %convolution_convert_fusion = bf16[1536,768]{1,0:T(8,128)(2,1)} fusion(bf16[1024,768]{1,0:T(8,128)(2,1)S(1)} %copy-done.20, f32[1024,1536]{1,0:T(8,128)} %copy-done.48, f32[1536]{0:T(1024)S(1)} %copy-done.45), kind=kOutput, calls=%fused_computation.34 | convolution fusion | flops 2432827392 | bytes 10229760 | tf_op jit(solution)/shard_map/tf,td->fd/dot_general | solution.py:603
  338.5 1.0 convolution_convert_fusion.7
  339.6 0.9 slice.62
  340.4 1.0 copy-done.41
  341.4 4.0 convolution_convert_fusion.2
  346.5 1.4 pad_maximum_fusion
  347.9 2.1 reduce_sum.155
  350.1 0.8 slice.50
  351.2 53.1 %all-reduce.22.cloned.1.call-done = (bf16[1024,768]{1,0:T(8,128)(2,1)}, bf16[1024,768]{1,0:T(8,128)(2,1)}) async-done(((bf16[1024,768]{1,0:T(8,128)(2,1)}, bf16[1024,768]{1,0:T(8,128)(2,1)}), (bf16[1024,768]{1,0:T(8,128)(2,1)}, bf16[1024,768]{1,0:T(8,128)(2,1)})) %all-reduce.22.cloned.1.call-update) | async-done | bytes 3145744 | tf_op jit(solution)/shard_map/psum | solution.py:597
  404.2 2.7 add_add_fusion.3
  406.9 4.1 copy.44
  411.0 5.4 reshape.178
  416.4 3.0 convert_reduce_fusion
  419.5 2.1 fusion.20
  421.6 1.8 add_add_fusion.2
  423.4 4.1 copy.47
  427.5 5.3 reshape.183
  432.8 63.7 %all-reduce.8 = (f32[768]{0:T(1024)}, f32[768]{0:T(1024)}, f32[2,384]{1,0:T(2,128)}, f32[768]{0:T(1024)}, f32[768]{0:T(1024)}, /*index=5*/f32[768]{0:T(1024)}, f32[1536]{0:T(1024)}, f32[768]{0:T(1024)}) all-reduce(f32[768]{0:T(1024)S(1)} %get-tuple-element.34, ...), channel_id=1, replica_groups=mesh['seq'=16,'heads'=2] {'seq'}, use_global_device_ids=true, to_apply=%region_13.14 | all-reduce | flops 6912 | bytes 55296 | tf_op jit(solution)/shard_map/psum | solution.py:639
  496.5 65.5 %all-reduce.20.cloned.1.call-done = (bf16[768,3,384]{2,0,1:T(8,128)(2,1)}, bf16[384,768]{1,0:T(8,128)(2,1)}, bf16[768,1536]{1,0:T(8,128)(2,1)}, bf16[1536,768]{1,0:T(8,128)(2,1)}) async-done(((bf16[768,3,384]{2,0,1:T(8,128)(2,1)}, bf16[384,768]{1,0:T(8,128)(2,1)}, bf16[768,1536]{1,0:T(8,128)(2,1)}, bf16[1536,768]{1,0:T(8,128)(2,1)}), (bf16[768,3,384]{2,0,1:T(8,128)(2,1)}, bf16[384,768]{1,0:T(8,128)(2,1)}, ...) | async-done | bytes 7077904 | tf_op jit(solution)/shard_map/psum | solution.py:638
  562.0 2.3 convert_element_type.146
  564.3 3.5 convert_element_type.144
  567.8 2.8 convert_element_type.148
  570.6 2.5 convert_element_type.150
  (129 shorter events, 5.5 us)
Async XLA Ops:
  7.2 165.4 %copy-start = (bf16[1536,768]{1,0:T(8,128)(2,1)S(1)}, bf16[1536,768]{1,0:T(8,128)(2,1)}, u32[]{:S(2)}) copy-start(bf16[1536,768]{1,0:T(8,128)(2,1)} %param.28) | copy-start | bytes 7077892
  7.2 156.9 %all-reduce.16.cloned.1.call-start = ((), (), s32[]{:S(2)}) async-start(), calls=%async_computation | async-start | bytes 3145728 | tf_op jit(solution)/shard_map/psum | solution.py:587
  16.8 4.4 copy-start.5
  21.3 4.1 copy-start.39
  21.3 4.1 copy-start.40
  27.4 4.4 copy-start.35
  28.0 8.5 %copy-start.25 = (f32[768]{0:T(1024)S(1)}, f32[768]{0:T(1024)}, u32[]{:S(2)}) copy-start(f32[768]{0:T(1024)} %param.18) | copy-start | bytes 9220
  31.9 2.4 copy-start.34
  34.2 4.7 copy-start.21
  35.7 10.9 %copy-start.32 = (f32[1024]{0:T(1024)}, f32[1024]{0:T(1024)S(1)}, u32[]{:S(2)}) copy-start(f32[1024]{0:T(1024)S(1)} %add.142) | copy-start | bytes 12292
  35.7 4.5 copy-start.23
  39.0 1.2 copy-start.17
  46.5 57.9 %copy-start.15 = (bf16[384,768]{1,0:T(8,128)(2,1)S(1)}, bf16[384,768]{1,0:T(8,128)(2,1)}, u32[]{:S(2)}) copy-start(bf16[384,768]{1,0:T(8,128)(2,1)} %param.22) | copy-start | bytes 1769476
  107.9 129.2 %all-reduce.18.cloned.1.call-start = ((), (), s32[]{:S(2)}) async-start(), calls=%async_computation.1 | async-start | bytes 3145728 | tf_op jit(solution)/shard_map/psum | solution.py:609
  116.8 1.7 copy-start.6
  118.4 45.6 %copy-start.38 = (f32[768]{0:T(1024)S(1)}, f32[768]{0:T(1024)}, u32[]{:S(2)}) copy-start(f32[768]{0:T(1024)} %param.23) | copy-start | bytes 9220
  166.9 1.7 copy-start.3
  166.9 2.3 copy-start.26
  166.9 2.8 copy-start.42
  166.9 2.8 copy-start.46
  167.4 0.6 copy-start.30
  168.6 0.6 copy-start.28
  169.7 2.8 copy-start.19
  169.7 2.8 copy-start.44
  172.6 7.4 %copy-start.48 = (f32[1024,1536]{1,0:T(8,128)}, f32[1024,1536]{1,0:T(8,128)S(1)}, u32[]{:S(2)}) copy-start(f32[1024,1536]{1,0:T(8,128)S(1)} %fusion.40) | copy-start | bytes 18874372
  180.0 1.7 copy-start.49
  185.4 218.9 %all-reduce.22.cloned.1.call-start = ((), (), s32[]{:S(2)}) async-start(), calls=%async_computation.3 | async-start | bytes 6291456 | tf_op jit(solution)/shard_map/psum | solution.py:597
  186.8 50.2 %copy-start.27 = (f32[768]{0:T(1024)S(1)}, f32[768]{0:T(1024)}, u32[]{:S(2)}) copy-start(f32[768]{0:T(1024)} %param.24) | copy-start | bytes 9220
  194.7 45.8 %copy-start.31 = (f32[1024]{0:T(1024)S(1)}, f32[1024]{0:T(1024)}, u32[]{:S(2)}) copy-start(f32[1024]{0:T(1024)} %copy-done.30) | copy-start | bytes 12292
  194.7 45.9 %copy-start.29 = (f32[1024]{0:T(1024)S(1)}, f32[1024]{0:T(1024)}, u32[]{:S(2)}) copy-start(f32[1024]{0:T(1024)} %copy-done.28) | copy-start | bytes 12292
  237.0 3.6 copy-start.4
  237.0 3.8 copy-start.9
  240.6 2.3 copy-start.7
  242.9 1.6 copy-start.16
  244.5 3.2 copy-start.10
  247.7 65.8 %copy-start.22 = (bf16[768,8,48]{0,2,1:T(8,128)(2,1)S(1)}, bf16[768,8,48]{0,2,1:T(8,128)(2,1)}, u32[]{:S(2)}) copy-start(bf16[768,8,48]{0,2,1:T(8,128)(2,1)} %copy-done.21) | copy-start | bytes 1769476
  247.7 65.8 %copy-start.24 = (bf16[768,8,48]{0,2,1:T(8,128)(2,1)S(1)}, bf16[768,8,48]{0,2,1:T(8,128)(2,1)}, u32[]{:S(2)}) copy-start(bf16[768,8,48]{0,2,1:T(8,128)(2,1)} %get-tuple-element.67) | copy-start | bytes 1769476
  321.2 0.7 copy-start.47
  321.2 8.9 %copy-start.20 = (bf16[1024,768]{1,0:T(8,128)(2,1)S(1)}, bf16[1024,768]{1,0:T(8,128)(2,1)}, u32[]{:S(2)}) copy-start(bf16[1024,768]{1,0:T(8,128)(2,1)} %bitcast_convert_fusion.1) | copy-start | bytes 4718596
  321.2 8.9 %copy-start.45 = (f32[1536]{0:T(1024)S(1)}, f32[1536]{0:T(1024)}, u32[]{:S(2)}) copy-start(f32[1536]{0:T(1024)} %param.27) | copy-start | bytes 18436
  321.2 240.7 %all-reduce.20.cloned.1.call-start = ((), (), s32[]{:S(2)}) async-start(), calls=%async_computation.2 | async-start | bytes 14155776 | tf_op jit(solution)/shard_map/psum | solution.py:638
  330.1 8.4 %copy-start.11 = (f32[1024,768]{1,0:T(8,128)S(1)}, f32[1024,768]{1,0:T(8,128)}, u32[]{:S(2)}) copy-start(f32[1024,768]{1,0:T(8,128)} %copy-done.10) | copy-start | bytes 9437188
  330.1 8.4 %copy-start.43 = (bf16[1024,512]{1,0:T(8,128)(2,1)S(1)}, bf16[1024,512]{1,0:T(8,128)(2,1)}, u32[]{:S(2)}) copy-start(bf16[1024,512]{1,0:T(8,128)(2,1)} %get-tuple-element.23) | copy-start | bytes 3145732
  338.5 1.9 copy-start.18
  338.5 2.9 copy-start.41
  347.9 56.3 %copy-start.37 = (f32[768]{0:T(1024)S(1)}, f32[768]{0:T(1024)}, u32[]{:S(2)}) copy-start(f32[768]{0:T(1024)} %param.29) | copy-start | bytes 9220
  411.0 5.4 copy-start.8
  416.4 3.1 copy-start.33
  416.4 3.1 copy-start.2
  419.4 2.2 copy-start.12
  427.5 5.3 copy-start.36
  561.9 5.8 %copy-start.14 = (bf16[768,1536]{1,0:T(8,128)(2,1)S(1)}, bf16[768,1536]{1,0:T(8,128)(2,1)}, u32[]{:S(2)}) copy-start(bf16[768,1536]{1,0:T(8,128)(2,1)} %get-tuple-element.52) | copy-start | bytes 7077892
  567.8 2.8 copy-start.13
  570.6 2.6 copy-start.1
Sparse Core Ops, SparseCore 0:
  108.0 55.9 all-reduce.15
  185.5 51.4 all-reduce.17
  321.3 82.8 all-reduce.21
  409.9 152.0 all-reduce.19

commit v2 on v1

--- a/solution.py
+++ b/solution.py
@@ -65,16 +65,32 @@
         place = (self.y * LOCAL + head) % stride
         return pl.multiple_of(reversed_bits(place, b) * (SEGMENT // stride), SEGMENT // stride)
 
-    def greet(self):
+    def bit(self, k):
+        return self.me // 2**k % 2
+
+    def partner(self, k):
+        return (self.me + 2**k * (1 - 2 * self.bit(k)), self.y)
+
+    def low(self, k):
+        return sum((self.bit(i) * HALVES[i] for i in range(k)), self.me * 0)
+
+    def greet(self, seq=16, other=False):
         barrier = pltpu.get_barrier_semaphore()
         i = self.member(4)
+        count = 15
+        if other:
+            pl.semaphore_signal(barrier, inc=1, device_id=(self.me, 1 - self.y), device_id_type=MESH)
+            count += 1
+        for k in far_bits(seq):
+            pl.semaphore_signal(barrier, inc=1, device_id=self.partner(k), device_id_type=MESH)
+            count += 1
 
         def signal(d, _):
             pl.semaphore_signal(barrier, inc=1, device_id=self.device(4, (i + d) % 16), device_id_type=MESH)
             return 0
 
         lax.fori_loop(1, 16, signal, 0)
-        pl.semaphore_wait(barrier, 15)
+        pl.semaphore_wait(barrier, count)
 
 
 def remote(src, dst, send, recv, device):
@@ -258,12 +274,134 @@
         over_peers(b, lambda d, t: back(b, d, t).wait_send())
 
 
+ROWS = 768
+HALVES = (384, 192, 96, 48)
+LANDING = (0, 384, 576, 672, 720)
+
+
+def far_bits(seq):
+    return list(range(4, seq.bit_length() - 1))
+
+
+class Halving:
+    def __init__(self, place, seq, pieces, grads, shares, scratch):
+        self.place, self.seq, self.pieces, self.grads, self.shares = place, seq, pieces, grads, shares
+        self.landing, self.send, self.recv, self.far_send, self.far_recv = scratch
+
+    @staticmethod
+    def scratch(seq, pieces):
+        far = len(far_bits(seq))
+        return (
+            [pltpu.VMEM((pieces, 720 + 48 * far, ROWS), BF)]
+            + [pltpu.SemaphoreType.DMA((pieces * 4,)) for _ in range(2)]
+            + [pltpu.SemaphoreType.DMA((pieces * max(far, 1),)) for _ in range(2)]
+        )
+
+    def copy(self, c, k):
+        size = HALVES[k]
+        start = self.place.low(k) + (1 - self.place.bit(k)) * size
+        return remote(
+            self.grads.at[c, pl.ds(pl.multiple_of(start, 48), size), :],
+            self.landing.at[c, pl.ds(LANDING[k], size), :],
+            self.send.at[c * 4 + k],
+            self.recv.at[c * 4 + k],
+            self.place.partner(k),
+        )
+
+    def add(self, c, k):
+        start = self.place.low(k + 1)
+
+        def step(i, _):
+            rows = pl.ds(pl.multiple_of(start + i * 48, 48), 48)
+            arrived = self.landing[c, pl.ds(pl.multiple_of(LANDING[k] + i * 48, 48), 48), :]
+            value = (self.grads[c, rows, :].astype(F32) + arrived.astype(F32)).astype(BF)
+            if k < 3:
+                self.grads[c, rows, :] = value
+            else:
+                self.shares[c] = value
+            return 0
+
+        lax.fori_loop(0, HALVES[k] // 48, step, 0)
+
+    def step(self, c, k):
+        if k > 0:
+            self.copy(c, k - 1).wait_recv()
+            self.add(c, k - 1)
+        if k < 4:
+            self.copy(c, k).start()
+            return
+        bits = far_bits(self.seq)
+        for n, bit in enumerate(bits):
+            at = pl.ds(720 + 48 * n, 48)
+            copy = remote(
+                self.shares.at[c],
+                self.landing.at[c, at, :],
+                self.far_send.at[c * len(bits) + n],
+                self.far_recv.at[c * len(bits) + n],
+                self.place.partner(bit),
+            )
+            copy.start()
+            copy.wait()
+            self.shares[c] = (self.shares[c].astype(F32) + self.landing[c, at, :].astype(F32)).astype(BF)
+
+    def finish(self):
+        def piece(c, _):
+            for k in range(4):
+                self.copy(c, k).wait_send()
+            return 0
+
+        lax.fori_loop(0, self.pieces, piece, 0)
+
+
+class Doubling:
+    def __init__(self, place, pieces, shares, result, sems, first=0):
+        self.place, self.pieces, self.shares, self.result, self.first = place, pieces, shares, result, first
+        self.send, self.recv = sems
+
+    @staticmethod
+    def scratch(pieces):
+        return [pltpu.SemaphoreType.DMA((pieces * 4,)) for _ in range(2)]
+
+    def copy(self, c, k):
+        rows = pl.ds(pl.multiple_of(self.place.low(k + 1), 48), HALVES[k])
+        view = self.result.at[self.first + c, rows, :]
+        return remote(view, view, self.send.at[c * 4 + k], self.recv.at[c * 4 + k], self.place.partner(k))
+
+    def step(self, c, k):
+        if k == 0:
+            rows = pl.ds(pl.multiple_of(self.place.low(4), 48), 48)
+            self.result[self.first + c, rows, :] = self.shares[c]
+        else:
+            self.copy(c, 4 - k).wait_recv()
+        if k < 4:
+            self.copy(c, 3 - k).start()
+
+    def finish(self):
+        def piece(c, _):
+            for k in range(4):
+                self.copy(c, k).wait_send()
+            return 0
+
+        lax.fori_loop(0, self.pieces, piece, 0)
+
+
+def run_at(slot, work, table):
+    for k in range(len(table[0])):
+        c = sum((jnp.where(slot == times[k], n + 1, 0) for n, times in enumerate(table)), slot * 0)
+
+        @pl.when(c > 0)
+        def _():
+            work.step(c - 1, k)
+
+
 def sem_shapes(per_copy):
     counts = [4, 6, 7, 15 * per_copy]
     return [pltpu.SemaphoreType.DMA((c,)) for c in counts]
 
 
 VMEM = pl.BlockSpec(memory_space=pltpu.VMEM)
+ANY = pl.BlockSpec(memory_space=pl.ANY)
+ORDER = tuple(int(f"{c:04b}"[::-1], 2) for c in range(16))
 
 
 def attention_forward(x):
@@ -318,11 +456,35 @@
     return total.T
 
 
+def put_48(pieces, head, value):
+    lane = lanes(value.shape)
+    at = head * 48
+    tile, off = at // 128, at % 128
+    value = jnp.where(lane < 48, value, 0.0)
+    if off:
+        value = pltpu.roll(value, off, 1)
+    if off + 48 > 128:
+        parts = [(tile, jnp.where(lane >= off, value, 0.0)), (tile + 1, jnp.where(lane < off - 80, value, 0.0))]
+    else:
+        parts = [(tile, value)]
+    for k, part in parts:
+        pieces[k] = part if pieces[k] is None else pieces[k] + part
+
+
 def backward_kernel(
-    x_ref, x1, x2, x3, q4, kv4, fin_ref, do_ref, g_ref, sum_ref,
-    d0, d1, d2, d3, d4, total, g1, g2, g3, gq4, gkv4, r1, r2, r3, rq4, rkv4, *sems
+    seq, x_ref, x1, x2, x3, q4, kv4, fin_ref, do_ref, ffn_ref, grads_in, g_ref, sum_ref, ffn_other, shares_ref,
+    grads, d0, d1, d2, d3, d4, total, g1, g2, g3, gq4, gkv4, r1, r2, r3, rq4, rkv4, *sems
 ):
     place = Place()
+    *sems, fill_sem, ffn_send, ffn_recv = sems
+    halving = Halving(place, seq, 4, grads, shares_ref, sems[16:])
+
+    def reduce_at(slot):
+        run_at(slot, halving, ((0, 1, 4, 5, 6), (2, 3, 6, 7, 8), (8, 9, 12, 13, 14), (10, 11, 14, 15, 16)))
+
+    for c in range(4):
+        pltpu.make_async_copy(grads_in.at[c], grads.at[c], fill_sem.at[c]).start()
+    ffn_copy = remote(ffn_ref, ffn_other, ffn_send, ffn_recv, (place.me, 1 - place.y))
     me = place.me
     xs, dd, gs, rs = (None, x1, x2, x3), (None, d1, d2, d3), (None, g1, g2, g3), (None, r1, r2, r3)
     go_send, go_recv, back_send, back_recv = sems[0:4], sems[4:8], sems[8:12], sems[12:16]
@@ -389,9 +551,12 @@
         return 0
 
     lax.fori_loop(0, LOCAL, prepare, 0)
-    place.greet()
+    place.greet(seq, True)
     for b in (4, 3, 2, 1):
         over_peers(b, lambda d, t: go(b, d, t).start())
+    ffn_copy.start()
+    for c in range(4):
+        pltpu.make_async_copy(grads_in.at[c], grads.at[c], fill_sem.at[c]).wait()
     for b in (1, 2, 3):
         n, tiles = SEGMENT // 2**b, LOCAL // 2**b
         i = place.member(b)
@@ -408,6 +573,7 @@
         total[h, :, 0:128] = pair_grads(
             x_ref[h, :, 0:128], d0[h], lambda half: x_ref[h, pl.ds(half * 512, 512), 128:256], put
         )
+        reduce_at(jnp.where(h < 4, h, h + 8))
         return 0
 
     lax.fori_loop(0, 4, local_head, 0)
@@ -421,6 +587,8 @@
     over_peers(4, lambda d, t: [c.start() for c in back(4, d, t)])
     rq4[i // 2, ds(i % 2 * 32, 32), :] = gq4[ds(i * 32, 32), :]
     rkv4[i % 2, i // 2] = gkv4[ds(i * 64, 64), :]
+    reduce_at(jnp.int32(4))
+    slot = 5
     for b in (3, 2, 1):
         n, tiles = SEGMENT // 2**b, LOCAL // 2**b
         over_peers(b, lambda d, t: go(b, d, t).wait_recv())
@@ -432,9 +600,11 @@
             gs[b][t, :, 0:128] = pair_grads(
                 xs[b][t, :, 0:128], dd[b][t], lambda half: xs[b][t, pl.ds(half * 512, 512), 128:256], put
             ).astype(BF)
+            reduce_at(slot + t)
             return 0
 
         lax.fori_loop(0, tiles, tile, 0)
+        slot += tiles
         over_peers(b, lambda d, t: [c.start() for c in back(b, d, t)])
         j = place.member(b)
         for t in range(tiles):
@@ -453,33 +623,47 @@
         rows = pl.ds(place.start(4, h), 64)
         total[h, rows, 0:128] += rq4[h].astype(F32)
         total[h, rows, 128:256] += rkv4[0, h].astype(F32) + rkv4[1, h].astype(F32)
-        grad = total[h]
-        lane = lanes(grad.shape)
-        live = (x_ref[h, :, 176:177].astype(F32) >= 0.0).astype(F32)
-        key_factor = live * (1.0 / LOG2E)
-        grad = jnp.where(
-            lane < 48,
-            grad * SCALE,
-            jnp.where(
-                (lane >= 128) & (lane < 176),
-                grad * key_factor,
-                jnp.where((lane >= 192) & (lane < 240), grad, 0.0),
-            ),
-        )
-        g_ref[h] = grad.astype(BF)
-        sum_ref[h] = jnp.broadcast_to(jnp.sum(grad, axis=0, keepdims=True), (8, 256))
         return 0
 
     lax.fori_loop(0, LOCAL, finish, 0)
+    reduce_at(jnp.int32(16))
+    sum_ref[...] = jnp.zeros_like(sum_ref)
+
+    def compact(i, _):
+        rows = ds(i * 256, 256)
+        pieces = [[None] * 3 for _ in range(3)]
+        for h in range(LOCAL):
+            live = (x_ref[h, rows, 176:177].astype(F32) >= 0.0).astype(F32)
+            grad_kv = total[h, rows, 128:256]
+            put_48(pieces[0], h, total[h, rows, 0:128] * SCALE)
+            put_48(pieces[1], h, grad_kv * (live * (1.0 / LOG2E)))
+            put_48(pieces[2], h, pltpu.roll(grad_kv, 64, 1))
+        for k in range(3):
+            for n in range(3):
+                at = pl.ds(n * 128, 128)
+                g_ref[k, rows, at] = pieces[k][n].astype(BF)
+                sum_ref[k, :, at] += jnp.broadcast_to(jnp.sum(pieces[k][n], axis=0, keepdims=True), (8, 128))
+        return 0
+
+    lax.fori_loop(0, 4, compact, 0)
 
     for b in (4, 3, 2, 1):
         over_peers(b, lambda d, t: go(b, d, t).wait_send())
         over_peers(b, lambda d, t: [c.wait_send() for c in back(b, d, t)])
-
-
-def attention_backward(x, saved, fin, grad_out):
-    shapes = [((LOCAL, SEGMENT, 256), BF), ((LOCAL, 8, 256), F32)]
+    halving.finish()
+    ffn_copy.wait()
+
+
+def attention_backward(x, saved, fin, grad_out, ffn_part, grads):
+    seq = lax.axis_size("seq")
+    shapes = [
+        ((3, SEGMENT, LOCAL * HEAD_DIM), BF),
+        ((3, 8, LOCAL * HEAD_DIM), F32),
+        (ffn_part.shape, BF),
+        ((4, 48, ROWS), BF),
+    ]
     scratch = [
+        (grads.shape, BF),
         ((LOCAL, SEGMENT, 128), BF),
         ((4, SEGMENT, 128), BF),
         ((2, SEGMENT, 128), BF),
@@ -498,17 +682,195 @@
         ((2, LOCAL, 64, 128), BF),
     ]
     return pl.pallas_call(
-        backward_kernel,
+        functools.partial(backward_kernel, seq),
         out_shape=[jax.ShapeDtypeStruct(*s) for s in shapes],
-        in_specs=[VMEM] * 8,
-        out_specs=[VMEM] * len(shapes),
+        in_specs=[VMEM] * 8 + [ANY] * 2,
+        out_specs=[VMEM, VMEM, ANY, VMEM],
         scratch_shapes=[pltpu.VMEM(*s) for s in scratch]
-        + sem_shapes(1) + sem_shapes(1) + sem_shapes(2) + sem_shapes(2),
+        + sem_shapes(1) + sem_shapes(1) + sem_shapes(2) + sem_shapes(2)
+        + Halving.scratch(seq, 4)
+        + [pltpu.SemaphoreType.DMA((4,)), pltpu.SemaphoreType.DMA, pltpu.SemaphoreType.DMA],
         compiler_params=pltpu.CompilerParams(
             collective_id=1, has_side_effects=True, vmem_limit_bytes=60 * 2**20
         ),
         name="attention_backward",
-    )(x, *saved, fin, grad_out)
+    )(x, *saved, fin, grad_out, ffn_part, grads)
+
+
+CHUNK = 128
+
+
+def put_spread(planes, block, value):
+    for t in range(value.shape[1] // 128):
+        planes[t, pl.ds(ORDER[block], 64, stride=16), :] = value[:, t * 128 : (t + 1) * 128]
+
+
+def from_planes(planes, out):
+    def step(i, _):
+        rows = ds(i * 128, 128)
+        for t in range(planes.shape[0]):
+            out[rows, pl.ds(t * 128, 128)] = planes[t, rows, :]
+        return 0
+
+    lax.fori_loop(0, SEGMENT // 128, step, 0)
+
+
+def last_kernel(
+    seq, g_ref, w_ref, normed_ref, tokens_ref, middle_ref, gain_ref, w_out_ref, small_ref, shares_in,
+    out_ref, grads_ref, early_ref, late_ref,
+    grads, shares, part, other, early_in, late, late_in, sums, planes, part_send, part_recv, early_send, early_recv, late_send, late_recv,
+    *sems
+):
+    place = Place()
+    halving = Halving(place, seq, 2, grads, shares, sems[0:5])
+    gathers = Doubling(place, 4, shares_in, grads_ref, sems[5:7])
+    last_gathers = Doubling(place, 2, shares, grads_ref, sems[7:9], 4)
+    far_send, far_recv = sems[9:]
+    i = place.member(4)
+    chunks = SEGMENT // CHUNK
+
+    def to_all(src, landing, send, recv):
+        def each(action):
+            def step(d, _):
+                action(remote(src, landing.at[i], send.at[d - 1], recv.at[d - 1], place.device(4, (i + d) % 16)))
+                return 0
+
+            lax.fori_loop(1, 16, step, 0)
+
+        return each
+
+    def total_of(src, landing):
+        def step(j, value):
+            return value + landing[j]
+
+        landing[i] = src[...]
+        return lax.fori_loop(1, 16, step, landing[0])
+
+    def far_total(result, n):
+        for k, bit in enumerate(far_bits(seq)):
+            landing = (early_in, late_in)[n].at[16 + k]
+            copy = remote(result, landing, far_send.at[n * 8 + k], far_recv.at[n * 8 + k], place.partner(bit))
+            copy.start()
+            copy.wait()
+            result[...] = result[...] + landing[...]
+
+    def exchange(n):
+        rows = ds(n * CHUNK, CHUNK)
+        return remote(
+            part.at[rows, :], other.at[rows, :], part_send.at[n], part_recv.at[n], (place.me, 1 - place.y)
+        )
+
+    def partial(n, _):
+        rows = ds(n * CHUNK, CHUNK)
+        value = dot(g_ref[0, rows, :], w_ref[0], NT)
+        value += dot(g_ref[1, rows, :], w_ref[1], NT)
+        value += dot(g_ref[2, rows, :], w_ref[2], NT)
+        part[rows, :] = value.astype(BF)
+        exchange(n).start()
+        return 0
+
+    place.greet(seq, True)
+    lax.fori_loop(0, 2, partial, 0)
+    early_all = to_all(small_ref, early_in, early_send, early_recv)
+    early_all(lambda copy: copy.start())
+    for k in range(3):
+        at = pl.ds(k % 2 * 384, 384)
+        grads[k // 2, :, at] = dot(normed_ref[...], g_ref[k], TN).astype(BF)
+        if k == 1:
+            halving.step(0, 0)
+    grads[1, :, pl.ds(384, 384)] = w_out_ref[...]
+    halving.step(1, 0)
+    lax.fori_loop(2, chunks, partial, 0)
+    sums[...] = jnp.zeros_like(sums)
+
+    for n in range(chunks):
+        exchange(n).wait_recv()
+        for block in range(CHUNK // 64):
+            b = n * (CHUNK // 64) + block
+            rows = pl.ds(b * 64, 64)
+            x = tokens_ref[rows, :].astype(F32)
+            centered = x - jnp.mean(x, axis=1, keepdims=True)
+            rs = lax.rsqrt(jnp.mean(centered * centered, axis=1, keepdims=True) + layer_eps)
+            xhat = centered * rs
+            grad = part[rows, :].astype(F32) + other[rows, :].astype(F32)
+            sums[0:8] += jnp.sum((grad * xhat).reshape(8, 8, -1), axis=0)
+            sums[8:16] += jnp.sum(grad.reshape(8, 8, -1), axis=0)
+            grad = grad * gain_ref[...]
+            grad = grad - jnp.mean(grad, axis=1, keepdims=True) - xhat * jnp.mean(grad * xhat, axis=1, keepdims=True)
+            put_spread(planes, b, middle_ref[rows, :] + rs * grad)
+        for c in range(2):
+            if 1 <= n + 1 - c <= 4:
+                halving.step(c, n + 1 - c)
+            if 0 <= n - 3 - c <= 4:
+                last_gathers.step(c, n - 3 - c)
+        for c in range(4):
+            if 0 <= n - c <= 4:
+                gathers.step(c, n - c)
+    for k in range(2):
+        value = jnp.sum(sums[k * 8 : k * 8 + 8], axis=0, keepdims=True)
+        for t in range(6):
+            late[pl.ds(k * 8 + t, 1), :] = value[:, t * 128 : (t + 1) * 128]
+        late[pl.ds(k * 8 + 6, 2), :] = jnp.zeros((2, 128), F32)
+    late_all = to_all(late, late_in, late_send, late_recv)
+    late_all(lambda copy: copy.start())
+    last_gathers.step(1, 4)
+    from_planes(planes, out_ref)
+    early_all(lambda copy: copy.wait_recv())
+    early_ref[...] = total_of(small_ref, early_in)
+    far_total(early_ref, 0)
+    late_all(lambda copy: copy.wait_recv())
+    late_ref[...] = total_of(late, late_in)
+    far_total(late_ref, 1)
+
+    def sent(n, _):
+        exchange(n).wait_send()
+        return 0
+
+    lax.fori_loop(0, chunks, sent, 0)
+    early_all(lambda copy: copy.wait_send())
+    late_all(lambda copy: copy.wait_send())
+    halving.finish()
+    gathers.finish()
+    last_gathers.finish()
+
+
+def last_part(g, w_project, normed, tokens, grad_middle, gain, grad_w_out, small, shares):
+    seq = lax.axis_size("seq")
+    far = len(far_bits(seq))
+    width = normed.shape[1]
+    shapes = [
+        (normed.shape, F32),
+        ((6, ROWS, ROWS), BF),
+        (small.shape, F32),
+        ((16, 128), F32),
+    ]
+    scratch = [
+        ((2, ROWS, ROWS), BF),
+        ((2, 48, ROWS), BF),
+        (normed.shape, BF),
+        (normed.shape, BF),
+        ((16 + far,) + small.shape, F32),
+        ((16, 128), F32),
+        ((16 + far, 16, 128), F32),
+        ((16, width), F32),
+        ((width // 128, SEGMENT, 128), F32),
+    ]
+    chunks = SEGMENT // CHUNK
+    counts = (chunks, chunks, 15, 15, 15, 15)
+    return pl.pallas_call(
+        functools.partial(last_kernel, seq),
+        out_shape=[jax.ShapeDtypeStruct(*s) for s in shapes],
+        in_specs=[VMEM] * 9,
+        out_specs=[VMEM] * len(shapes),
+        scratch_shapes=[pltpu.VMEM(*s) for s in scratch]
+        + [pltpu.SemaphoreType.DMA((c,)) for c in counts]
+        + Halving.scratch(seq, 2) + Doubling.scratch(4) + Doubling.scratch(2)
+        + [pltpu.SemaphoreType.DMA((16,)) for _ in range(2)],
+        compiler_params=pltpu.CompilerParams(
+            collective_id=2, has_side_effects=True, vmem_limit_bytes=56 * 2**20
+        ),
+        name="last_part",
+    )(g, w_project, normed, tokens, grad_middle, gain, grad_w_out, small, shares)
 
 
 def norm_rows(values, gain, shift):
@@ -520,9 +882,6 @@
 
 def gelu_tanh(values):
     return jax.nn.gelu(values, approximate=True)
-
-
-ORDER = tuple(int(f"{c:04b}"[::-1], 2) for c in range(16))
 
 
 def by_residue(rows):
@@ -593,11 +952,7 @@
     expand = jnp.dot(normed_two_low, w_expand, preferred_element_type=F32) + bias_expand
     active, undo_gelu = jax.vjp(gelu_tanh, expand)
     active_low = active.astype(BF)
-    reduced = (
-        lax.psum(jnp.dot(active_low, w_reduce, preferred_element_type=F32).astype(BF), "heads").astype(F32)
-        + bias_reduce
-    )
-    layer_out = middle + reduced
+    ffn_part = jnp.dot(active_low, w_reduce, preferred_element_type=F32).astype(BF)
     grad_bias_reduce = jnp.sum(cotangent, axis=0)
     cotangent_low = cotangent.astype(BF)
     grad_w_reduce = jnp.einsum("tf,td->fd", active_low, cotangent_low, preferred_element_type=F32)
@@ -617,53 +972,57 @@
         jnp.einsum("te,td->ed", attended, grad_middle_low, preferred_element_type=F32)
         .reshape(LOCAL, 64, width)[:, :HEAD_DIM]
         .reshape(-1, width)
+        .astype(BF)
     )
+    half = width // 2
+    grad_w_output = jnp.concatenate([grad_w_output[:, :half], grad_w_output[:, half:]], axis=0)
     grad_attended = jnp.einsum("td,ed->te", grad_middle_low, w_out_wide, preferred_element_type=F32).astype(BF)
-    early = lax.psum(
-        (grad_w_output.astype(BF), grad_w_expand.astype(BF), grad_w_reduce.astype(BF)), "seq"
+    grad_w_reduce, grad_w_expand = grad_w_reduce.astype(BF), grad_w_expand.astype(BF)
+    grads = jnp.stack(
+        [grad_w_reduce[:width], grad_w_reduce[width:], grad_w_expand[:, :width], grad_w_expand[:, width:]]
     )
 
-    g, g_sums = attention_backward(x, saved, fin, grad_attended)
-    g_sums = g_sums[:, 0]
-    grad_bias_project = jnp.stack([g_sums[:, 0:48].reshape(-1), g_sums[:, 192:240].reshape(-1)])
-    grad_w_wide = jnp.einsum("td,hte->dhe", normed_low, g, preferred_element_type=F32)
-    grad_w_project = jnp.stack(
-        [grad_w_wide[:, :, k : k + 48].reshape(width, -1) for k in (0, 128, 192)], axis=1
-    )
-    grad_normed = lax.psum(
-        jnp.einsum("hte,dhe->td", g, w_wide, preferred_element_type=F32).astype(BF), "heads"
-    ).astype(F32)
-    grad_inputs_part, grad_gain_first, grad_shift_first = undo_first(grad_normed)
-    grad_tokens = grad_middle + grad_inputs_part
-    grad_w_project = lax.psum(grad_w_project.astype(BF), "seq")
-    summed = lax.psum(
-        (
-            grad_gain_first,
-            grad_shift_first,
-            grad_bias_project,
+    g, g_sums, ffn_other, shares = attention_backward(x, saved, fin, grad_attended, ffn_part, grads)
+    layer_out = middle + (ffn_part.astype(F32) + ffn_other.astype(F32)) + bias_reduce
+    small = jnp.concatenate(
+        [
+            g_sums[0, 0],
+            g_sums[2, 0],
             grad_bias_output,
             grad_gain_second,
             grad_shift_second,
             grad_bias_expand,
             grad_bias_reduce,
-        ),
-        "seq",
+            jnp.zeros((6 * 128,), F32),
+        ]
+    ).reshape(48, 128)
+    grad_tokens, grads, small, late = last_part(
+        g, w_project.transpose(1, 0, 2), normed_low, tokens, grad_middle, gain_first[None], grad_w_output, small, shares
     )
+    small = small.reshape(-1)
+    grads = grads.astype(F32)
+    last_grads = grads[4:]
+    grad_w_project = jnp.stack(
+        [last_grads[0, :, :half], last_grads[0, :, half:], last_grads[1, :, :half]], axis=1
+    )
+    grad_w_output = jnp.concatenate([last_grads[1, :half, half:], last_grads[1, half:, half:]], axis=1)
+    late = late.reshape(2, 8 * 128)[:, :width]
+    parts = [small[k * width : (k + 1) * width] for k in range(7)]
     return (
         from_residue(layer_out),
-        from_residue(grad_tokens),
-        summed[0],
-        summed[1],
-        grad_w_project.astype(F32),
-        summed[2],
-        early[0].astype(F32),
-        summed[3],
-        summed[4],
-        summed[5],
-        early[1].astype(F32),
-        summed[6],
-        early[2].astype(F32),
-        summed[7],
+        grad_tokens,
+        late[0],
+        late[1],
+        grad_w_project,
+        parts[0].reshape(2, half),
+        grad_w_output,
+        parts[1],
+        parts[2],
+        parts[3],
+        jnp.concatenate([grads[2], grads[3]], axis=1),
+        small[4 * width : 6 * width],
+        jnp.concatenate([grads[0], grads[1]], axis=0),
+        parts[6],
     )
 
 

time: 589 us -> 501 us (0.85)
  waiting for transfers between devices: 205 us -> 80.4 us
  Pallas kernels: 124 us -> 247 us
  blocking collectives: 63.7 us -> 0 us
  matrix products: 64.2 us -> 46.7 us
    pallas_call x1 -> x2, Pallas kernels: 65.7 us -> 189 us  [the longest x1 101 us: attention_backward(): pl.pallas_call(functools.partial(backward_kernel, seq), out_shape=[jax.Sh...]
    psum x2 -> x0, waiting for transfers between devices: 119 us -> none  [the longest x1 65.5 us: body(): grad_w_project = lax.psum(grad_w_project.astype(BF), 'seq')]
    psum x1 -> x0, blocking collectives: 63.7 us -> none  [body(): lax.psum((grad_gain_first, grad_shift_first, grad_bias_project, grad_bias...]
    dot_general x2 -> x0, matrix products: 11.8 us -> none  [the longest x1 7.76 us: body(): jnp.einsum('hte,dhe->td', g, w_wide, preferred_element_type=F32).astype(BF)]
    concatenate x0 -> x4, other arithmetic: none -> 10.4 us  [the longest x1 4.31 us: body(): jnp.concatenate([grads[0], grads[1]], axis=0)]
    convert_element_type x2 -> x0, local copies, waits for them, and re-layouts: 8.34 us -> none  [body(): inputs = tokens.astype(F32)]
    reshape x2 -> x4, local copies, waits for them, and re-layouts: 8.84 us -> 16.9 us  [by_residue(): shaped = rows.reshape((rows.shape[0] // 16, 2, 2, 2, 2) + rows.shape[1:])]
    reshape x2 -> x1, local copies, waits for them, and re-layouts: 10.7 us -> 3.33 us  [from_residue(): return shaped.transpose((4, 3, 2, 1, 0) + rest).reshape(rows.shape)]
  transfers between devices with their start and end apart: 4 -> 2, of which waited for: 4 -> 2; matrix products, arithmetic and copies ran while one was open for 13% -> 5% of each run, Pallas kernels for 0% -> 0%
where the time goes in v2:
time: 501 us; the launch traced here: 492 us
  Pallas kernels  247 us (49%)
  waiting for transfers between devices  80.4 us (16%)
  local copies, waits for them, and re-layouts  57.4 us (11%)
  matrix products  46.7 us (9%)
  other arithmetic  45.7 us (9%)
  between operations  15 us (3%)
    pallas_call x1, Pallas kernels, attention_backward(): pl.pallas_call(functools.partial(backward_kernel, seq), out_shape=[jax.Sh...  101 us
    pallas_call x1, Pallas kernels, last_part(): pl.pallas_call(functools.partial(last_kernel, seq), out_shape=[jax.ShapeD...  88.7 us
    pallas_call x1, Pallas kernels, attention_forward(): pl.pallas_call(forward_kernel, out_shape=[jax.ShapeDtypeStruct(*s) for s...  57.4 us
    psum x1, waiting for transfers between devices, body(): lax.psum(jnp.einsum('tf,df->td', grad_expand_low, w_expand, preferred_ele...  41 us
    psum x1, waiting for transfers between devices, body(): lax.psum(jnp.dot(attended, w_out_rows, preferred_element_type=F32).astype...  39.4 us
    reshape x4, local copies, waits for them, and re-layouts, by_residue(): shaped = rows.reshape((rows.shape[0] // 16, 2, 2, 2, 2) + rows.shape[1:])  16.9 us
    unnamed x101, local copies, waits for them, and re-layouts  14.7 us
  transfers between devices with their start and end apart: 2, of which 2 were waited for; matrix products, arithmetic and copies ran while one was open for 5% of the time, Pallas kernels for 0%

profile of v2, /device:TPU:0, one launch (start us, length us, event | category | flops | bytes accessed | tf_op | source)
XLA Modules:
  0.0 492.0 jit_solution(9477852141504159682)
XLA Ops:
  7.3 4.6 reshape.166
  11.9 2.3 convert_reduce_fusion.1
  14.3 2.4 fusion.21
  16.7 3.0 copy.34
  20.0 0.4 convert_element_type.97
  20.4 0.2 copy.35
  20.8 3.9 copy.36
  24.7 1.7 slice_bitcast_fusion.15
  26.6 0.6 fusion.19.normed_ref
  27.3 1.2 copy-done.15
  28.5 5.7 %fusion.2.x_ref = bf16[8,1024,256]{2,1,0:T(8,128)(2,1)} fusion(f32[1024]{0:T(1024)S(1)} %convert_element_type.99, f32[8,256]{1,0:T(8,128)S(1)} %select_maximum_fusion, bf16[1024]{0:T(1024)(128)(2,1)S(1)} %subtract_multiply_fusion, pred[256]{0:T(512)(128)(4,1)S(1)} %get-tuple-element.85, pred[256]{0:T(512)(128)(4,1)S(1)} %get-tuple-element.84, ...), kind=kOutput, calls=%fused_computation.8 | convolution fusion | flops 3257925632 | bytes 7552000 | tf_op jit(solution)/shard_map/td,dhe->hte/dot_general | solution.py:936
  34.1 57.4 %attention_forward.1 = (f32[8,1024,128]{2,1,0:T(8,128)}, bf16[1024,512]{1,0:T(8,128)(2,1)}, bf16[4,1024,256]{2,1,0:T(8,128)(2,1)}, bf16[2,1024,256]{2,1,0:T(8,12...) custom-call(bf16[8,1024,256]{2,1,0:T(8,128)(2,1)} %fusion.2.x_ref), custom_call_target="tpu_custom_call" | custom-call | tf_op jit(solution)/shard_map/attention_forward/pallas_call | solution.py:429
  91.6 3.4 convolution_convert_fusion.3
  95.0 0.6 broadcast_in_dim.64.gain_ref
  95.6 1.3 pad.40
  96.9 2.7 reduce_sum.125
  99.6 5.3 %reshape.171 = f32[64,2,2,2,2,768]{5,4,3,2,1,0:T(2,128)} reshape(f32[1024,768]{1,0:T(8,128)} %param.16) | data formatting | bytes 6291456 | tf_op jit(solution)/shard_map/reshape | solution.py:888
  104.9 3.8 copy.38
  108.8 1.7 copy-done.5
  110.4 1.3 bitcast_convert_fusion
  111.7 39.4 %all-reduce.11.cloned.1.call-done = bf16[1024,768]{1,0:T(8,128)(2,1)} async-done(((bf16[1024,768]{1,0:T(8,128)(2,1)}), bf16[1024,768]{1,0:T(8,128)(2,1)}) %all-reduce.11.cloned.1.call-update) | async-done | bytes 1572880 | tf_op jit(solution)/shard_map/psum | solution.py:946
  151.1 2.6 fusion.35
  154.0 2.5 multiply_reduce_fusion
  156.5 4.7 fusion.54
  161.2 5.0 %convolution_convert_fusion.1 = bf16[1536,768]{1,0:T(8,128)(2,1)} fusion(bf16[1024,768]{1,0:T(8,128)(2,1)S(1)} %copy-done.24, f32[1024,1536]{1,0:T(8,128)S(1)} %fusion.54, f32[1536]{0:T(1024)S(1)} %copy-done.39), kind=kOutput, calls=%fused_computation.37 | convolution fusion | flops 2432827392 | bytes 10229760 | tf_op jit(solution)/shard_map/tf,td->fd/dot_general | solution.py:958
  166.3 7.4 %fusion.55 = (f32[1536]{0:T(1024)}, bf16[1024,1536]{1,0:T(8,128)(2,1)S(1)}) fusion(f32[1024,1536]{1,0:T(8,128)S(1)} %fusion.54, f32[1536]{0:T(1024)S(1)} %copy-done.39, bf16[1024,768]{1,0:T(8,128)(2,1)S(1)} %copy-done.24, bf16[1536,768]{1,0:T(8,128)(2,1)S(1)} %copy-done), kind=kOutput, calls=%fused_computation.140 | convolution fusion | flops 2450520576 | bytes 13381632 | tf_op jit(solution)/shard_map/td,fd->tf/dot_general | solution.py:959
  173.7 1.7 copy-done.43
  175.3 4.1 convolution_convert_fusion.4
  179.5 7.2 %convolution_convert_fusion = bf16[768,1536]{1,0:T(8,128)(2,1)} fusion(bf16[1024,1536]{1,0:T(8,128)(2,1)} %copy-done.43, f32[1024,768]{1,0:T(8,128)} %get-tuple-element.59, f32[768]{0:T(1024)S(1)} %copy-done.41, f32[768]{0:T(1024)S(1)} %copy-done.25, f32[1024]{0:T(1024)S(1)} %fusion.44), kind=kOutput, calls=%fused_computation.36 | convolution fusion | flops 2420244480 | bytes 8660992 | tf_op jit(solution)/shard_map/td,tf->df/dot_general | solution.py:963
  186.7 1.2 slice_bitcast_fusion.10
  187.9 1.9 slice_bitcast_fusion.8
  189.8 2.7 pad_maximum_fusion.grads_in
  192.5 1.0 slice-done.1
  193.5 5.0 %convolution_convert_fusion.5.ffn_ref = bf16[1024,768]{1,0:T(8,128)(2,1)} fusion(bf16[1536,768]{1,0:T(8,128)(2,1)S(1)} %copy-done, f32[1024,1536]{1,0:T(8,128)S(1)} %bitcast.100, f32[1536]{0:T(1024)S(1)} %copy-done.40), kind=kOutput, calls=%fused_computation.68 | convolution fusion | flops 2432434176 | bytes 10229760 | tf_op jit(solution)/shard_map/dot_general | solution.py:955
  198.5 41.0 %all-reduce.13.cloned.1.call-done = bf16[1024,768]{1,0:T(8,128)(2,1)} async-done(((bf16[1024,768]{1,0:T(8,128)(2,1)}), bf16[1024,768]{1,0:T(8,128)(2,1)}) %all-reduce.13.cloned.1.call-update) | async-done | bytes 1572880 | tf_op jit(solution)/shard_map/psum | solution.py:964
  239.5 3.2 convert_reduce_fusion
  242.8 3.2 fusion.22
  246.0 2.7 fusion.57
  248.8 1.1 convolution_convert_fusion.6
  250.0 0.4 copy-done.10
  250.4 0.9 copy-done.23
  251.3 3.2 convolution_convert_fusion.2.do_ref
  254.5 100.6 %attention_backward.1 = (bf16[3,1024,384]{2,1,0:T(8,128)(2,1)}, f32[3,8,384]{2,1,0:T(8,128)}, bf16[1024,768]{1,0:T(8,128)(2,1)}, bf16[4,48,768]{2,1,0:T(8,128)(2,1)}) custom-call(bf16[8,1024,256]{2,1,0:T(8,128)(2,1)} %fusion.2.x_ref, bf16[4,1024,256]{2,1,0:T(8,128)(2,1)} %get-tuple-element.30.x1, bf16[2,1024,256]{2,1,0:T(8,128)(2,1)} %get-tuple-element.31.x2, ...), custom_call_target="tpu_custom_call" | custom-call | tf_op jit(solution)/shard_map/attention_backward/pallas_call | solution.py:684
  355.1 0.7 slice_reduce_fusion.2
  356.0 0.9 pad_maximum_fusion.5.w_out_ref
  356.9 88.7 %last_part.1 = (f32[1024,768]{1,0:T(8,128)}, bf16[6,768,768]{2,1,0:T(8,128)(2,1)}, f32[48,128]{1,0:T(8,128)}, f32[16,128]{1,0:T(8,128)}) custom-call(bf16[3,1024,384]{2,1,0:T(8,128)(2,1)} %get-tuple-element.37.g_ref, bf16[3,768,384]{2,1,0:T(8,128)(2,1)} %bitcast.90, bf16[1024,768]{1,0:T(8,128)(2,1)} %copy-done.15, bf16[1024,768]{1,0:T(8,128)(2,1)} %bitcast.87, ...), custom_call_target="tpu_custom_call" | custom-call | tf_op jit(solution)/shard_map/last_part/pallas_call | solution.py:860
  445.6 1.3 slice_bitcast_fusion.16
  446.9 1.4 slice_bitcast_fusion.17
  448.3 4.3 convert_element_type.119
  452.6 1.1 slice_bitcast_fusion.12
  453.7 1.9 slice_bitcast_fusion.6
  455.6 4.7 slice_bitcast_fusion.1
  460.2 0.6 copy-done.14
  460.9 2.4 add_add_fusion.1
  463.3 2.4 copy.39
  465.8 3.3 reshape.175
  469.1 0.6 slice_reduce_fusion
  469.7 0.6 reshape.179
  470.3 2.3 pad_maximum_fusion.4
  472.7 4.3 pad_maximum_fusion.2
  477.0 2.9 pad_maximum_fusion.1
  479.9 2.0 pad_maximum_fusion.3
  481.9 1.1 copy-done.20
  483.1 1.7 copy.54
  (121 shorter events, 1.5 us)
Async XLA Ops:
  7.2 159.1 %copy-start = (bf16[1536,768]{1,0:T(8,128)(2,1)S(1)}, bf16[1536,768]{1,0:T(8,128)(2,1)}, u32[]{:S(2)}) copy-start(bf16[1536,768]{1,0:T(8,128)(2,1)} %param.28) | copy-start | bytes 7077892
  7.2 143.9 %all-reduce.11.cloned.1.call-start = ((), (), s32[]{:S(2)}) async-start(), calls=%async_computation | async-start | bytes 3145728 | tf_op jit(solution)/shard_map/psum | solution.py:946
  11.9 7.9 %copy-start.35 = (s32[1024]{0:T(1024)S(1)}, s32[1024]{0:T(1024)}, u32[]{:S(2)}) copy-start(s32[1024]{0:T(1024)} %param.17) | copy-start | bytes 12292
  11.9 7.9 %copy-start.36 = (f32[2,384]{1,0:T(2,128)S(1)}, f32[2,384]{1,0:T(2,128)}, u32[]{:S(2)}) copy-start(f32[2,384]{1,0:T(2,128)} %param.21) | copy-start | bytes 9220
  20.8 5.6 %copy-start.29 = (f32[768]{0:T(1024)S(1)}, f32[768]{0:T(1024)}, u32[]{:S(2)}) copy-start(f32[768]{0:T(1024)} %param.18) | copy-start | bytes 9220
  20.8 5.6 %copy-start.33 = (f32[768]{0:T(1024)S(1)}, f32[768]{0:T(1024)}, u32[]{:S(2)}) copy-start(f32[768]{0:T(1024)} %param.19) | copy-start | bytes 9220
  24.7 1.9 copy-start.2
  27.3 1.2 copy-start.15
  34.1 57.4 %copy-start.21 = (bf16[384,768]{1,0:T(8,128)(2,1)S(1)}, bf16[384,768]{1,0:T(8,128)(2,1)}, u32[]{:S(2)}) copy-start(bf16[384,768]{1,0:T(8,128)(2,1)} %param.22) | copy-start | bytes 1769476
  95.0 144.6 %all-reduce.13.cloned.1.call-start = ((), (), s32[]{:S(2)}) async-start(), calls=%async_computation.1 | async-start | bytes 3145728 | tf_op jit(solution)/shard_map/psum | solution.py:964
  108.7 1.7 copy-start.5
  110.4 40.7 %copy-start.26 = (f32[768]{0:T(1024)S(1)}, f32[768]{0:T(1024)}, u32[]{:S(2)}) copy-start(f32[768]{0:T(1024)} %param.23) | copy-start | bytes 9220
  151.1 2.6 copy-start.3
  151.1 2.8 copy-start.8
  154.0 2.5 copy-start.25
  154.0 2.5 copy-start.37
  154.0 2.5 copy-start.41
  156.5 4.7 copy-start.24
  156.5 4.7 copy-start.39
  161.2 5.0 %copy-start.42 = (f32[1024,1536]{1,0:T(8,128)}, f32[1024,1536]{1,0:T(8,128)S(1)}, u32[]{:S(2)}) copy-start(f32[1024,1536]{1,0:T(8,128)S(1)} %fusion.54) | copy-start | bytes 18874372
  173.7 1.7 copy-start.43
  179.4 7.2 %copy-start.22 = (bf16[1536,768]{1,0:T(8,128)(2,1)S(1)}, bf16[1536,768]{1,0:T(8,128)(2,1)}, u32[]{:S(2)}) copy-start(bf16[1536,768]{1,0:T(8,128)(2,1)} %convolution_convert_fusion.1) | copy-start | bytes 7077892
  187.9 2.0 copy-start.19
  187.9 4.7 slice-start
  189.8 2.7 copy-start.40
  189.8 3.7 slice-start.1
  239.5 3.3 copy-start.7
  242.7 3.3 copy-start.6
  246.0 2.7 copy-start.38
  248.8 1.7 copy-start.10
  248.8 2.5 copy-start.23
  254.5 101.4 %copy-start.27 = (f32[6144]{0:T(1024)S(1)}, f32[6144]{0:T(1024)}, u32[]{:S(2)}) copy-start(f32[6144]{0:T(1024)} %custom-call) | copy-start | bytes 73732
  254.5 101.5 %copy-start.31 = (f32[1536]{0:T(1024)S(1)}, f32[1536]{0:T(1024)}, u32[]{:S(2)}) copy-start(f32[1536]{0:T(1024)} %get-tuple-element.54) | copy-start | bytes 18436
  254.5 101.5 %copy-start.30 = (f32[768]{0:T(1024)S(1)}, f32[768]{0:T(1024)}, u32[]{:S(2)}) copy-start(f32[768]{0:T(1024)} %reduce_sum.125) | copy-start | bytes 9220
  356.0 0.9 copy-start.28
  455.5 4.7 copy-start.4
  455.6 4.7 copy-start.9
  455.6 5.3 %copy-start.14 = (bf16[1024,768]{1,0:T(8,128)(2,1)S(1)}, bf16[1024,768]{1,0:T(8,128)(2,1)}, u32[]{:S(2)}) copy-start(bf16[1024,768]{1,0:T(8,128)(2,1)} %convolution_convert_fusion.5.ffn_ref) | copy-start | bytes 4718596
  455.6 5.3 %copy-start.34 = (f32[768]{0:T(1024)S(1)}, f32[768]{0:T(1024)}, u32[]{:S(2)}) copy-start(f32[768]{0:T(1024)} %param.29) | copy-start | bytes 9220
  465.8 3.3 copy-start.32
  469.1 3.6 copy-start.13
  472.7 4.3 copy-start.11
  472.7 4.3 copy-start.12
  477.0 2.9 copy-start.16
  477.0 2.9 copy-start.17
  477.0 2.9 copy-start.18
  479.9 3.2 copy-start.20
  481.9 2.8 copy-start.1
Sparse Core Ops, SparseCore 0:
  95.1 56.0 all-reduce.10
  188.0 51.4 all-reduce.12
